TPU v7x, 256 devices: a whole 4x4x8 slice. The times are simulated.
256 devices in a mesh: dp: 32 (over y, z), tensor: 4 (over x), section: 2 (over core).
Axes of the slice: x: 4, y: 4, z: 8, core: 2. Of those that a mesh axis runs over, the one named last changes fastest.
Arguments:
- query_heads: bfloat16 [32768, 4, 8, 128], P('dp', 'tensor', 'section'), may hold values from -5 to 5, as said below
- key_heads: bfloat16 [32768, 4, 128], P('dp', 'tensor'), may hold values from -5 to 5, as said below
- value_heads: bfloat16 [32768, 4, 128], P('dp', 'tensor'), may hold values from -6 to 6
- attend_grad: bfloat16 [32768, 4, 8, 128], P('dp', 'tensor', 'section'), may hold values from -6 to 6
- doc_ids: int32 [32768], P('dp'), may hold values from 0 to 31, as said below
- cell_plan: int32 [512], P('dp'), may hold values from -1 to 31, as said below
Outputs:
- query_grad: bfloat16 [32768, 4, 8, 128], P('dp', 'tensor', 'section')
- key_grad: bfloat16 [32768, 4, 128], P('dp', 'tensor')
- value_grad: bfloat16 [32768, 4, 128], P('dp', 'tensor')
Inputs may be any that keep to these rules, and one draw needn't show every extreme that they name: `doc_ids`: never falling along a replica. In every cell of 64 tokens it changes exactly once, at the cell's fifth token or later; the cell's first token differs from the last token of the cell before it. `cell_plan`: in a quarter of the replicas the first 8 cells stay (-1) and the others are sent; in the other replicas every cell is sent. A sent cell has the value dest + slot: dest is the replica that receives it, which never keeps cells, and slot tells apart the cells of one replica that go to one replica. Some replica sends exactly 1 cell to one replica. Every replica receives at most 19 cells, and some receive exactly 19. `query_heads`: real values. `key_heads`: real values.
All inputs are finite; a program needn't handle non-finite values.
Results may differ from a plain program's by a relative error of at most 0.025.
Values may be sent and summed in bfloat16 or wider, within the bound.
A program may use at most 64 MiB of HBM per device.

v0:
```python
import functools

import jax
import jax.numpy as jnp
from jax import lax
from jax.experimental import pallas as pl
from jax.experimental.pallas import tpu as pltpu
from jax.sharding import PartitionSpec as P

LONG = 8
MESH = pl.DeviceIdType.MESH
LOG2E = 1.4426950408889634
NEG = -1e30
F32 = jnp.float32
BF16 = jnp.bfloat16


def rows_of(index, count):
    return pl.ds(pl.multiple_of(index * count, count), count)


def softmax_grads(keys, vals, quer, grad, mask, scale):
    nt = (((1,), (1,)), ((), ()))
    scores = lax.dot_general(keys, quer, nt, preferred_element_type=F32)
    scores = jnp.where(mask, scores, NEG)
    prob_grad = lax.dot_general(vals, grad, nt, preferred_element_type=F32)
    top = jnp.max(scores, axis=0, keepdims=True)
    unnorm = jnp.exp2((scores - top) * (scale * LOG2E))
    probs = unnorm * (1.0 / jnp.sum(unnorm, axis=0, keepdims=True))
    delta = jnp.sum(probs * prob_grad, axis=0, keepdims=True)
    dscore = (probs * (prob_grad - delta)).astype(BF16)
    dv = jnp.dot(probs.astype(BF16), grad, preferred_element_type=F32)
    dk = jnp.dot(dscore, quer, preferred_element_type=F32) * scale
    dq = (
        lax.dot_general(dscore, keys, (((0,), (0,)), ((), ())), preferred_element_type=F32)
        * scale
    )
    return dq, dk, dv


def kernel(
    n, cells, cell, long_cells, heads,
    info, q_ref, k_ref, v_ref, g_ref,
    dq_ref, dkv_ref,
    in1, out1, in2, out2, in3, out3, in4, out4,
    prev, dprev, dprev_rx, own, own_rx,
    send_sem, recv_sem, sib_send, sib_recv,
):
    me = lax.axis_index("dp")
    core = lax.axis_index("section")
    sib = 1 - core
    crow = cell * heads
    scale = q_ref.shape[-1] ** -0.5
    INV, BND = cells, cells + n

    barrier = pltpu.get_barrier_semaphore()

    def greet(k, _):
        pl.semaphore_signal(
            barrier, inc=1, device_id={"dp": lax.rem(me + k, n)}, device_id_type=MESH
        )
        return 0

    lax.fori_loop(1, n, greet, 0)
    pl.semaphore_signal(barrier, inc=1, device_id={"section": sib}, device_id_type=MESH)

    def hop(phase, src, dst, peer, slot):
        return pltpu.make_async_remote_copy(
            src_ref=src.at[peer],
            dst_ref=dst.at[slot],
            send_sem=send_sem.at[phase, peer],
            recv_sem=recv_sem.at[phase, slot],
            device_id={"dp": peer},
            device_id_type=MESH,
        )

    def arrived(phase, src, dst, peer):
        hop(phase, src, dst, peer, peer).wait_recv()

    def sent(phase, src, dst):
        def body(k, _):
            peer = lax.rem(me + k, n)
            hop(phase, src, dst, peer, peer).wait_send()
            return 0

        lax.fori_loop(1, n, body, 0)

    def swap(which, src, dst):
        return pltpu.make_async_remote_copy(
            src_ref=src,
            dst_ref=dst,
            send_sem=sib_send.at[which],
            recv_sem=sib_recv.at[which],
            device_id={"section": sib},
            device_id_type=MESH,
        )

    first_row = lax.broadcasted_iota(jnp.int32, (cell, k_ref.shape[-1]), 0) == 0

    def fill(d, _):
        at = info[INV + d]
        pos = jnp.maximum(at, 0)
        block = jnp.where(core == 0, k_ref[pos], v_ref[pos]).astype(F32)
        block = jnp.where(first_row, info[BND + pos].astype(F32), block)
        out1[d] = jnp.where(at >= 0, block, 0.0).astype(BF16)
        return 0

    lax.fori_loop(0, n, fill, 0)
    in1[me] = out1[me]

    pl.semaphore_wait(barrier, n)

    def launch1(k, _):
        hop(0, out1, in1, lax.rem(me + k, n), me).start()
        return 0

    lax.fori_loop(1, n, launch1, 0)

    long_len = long_cells * cell
    own[...] = jnp.zeros(own.shape, F32)
    dq_ref[long_cells * crow :, :] = jnp.zeros(
        (dq_ref.shape[0] - long_cells * crow, dq_ref.shape[1]), BF16
    )
    flat = (long_len, k_ref.shape[-1])
    long_key = lax.broadcasted_iota(jnp.int32, (long_len, crow), 0)
    long_query = lax.broadcasted_iota(jnp.int32, (long_len, crow), 1) // heads

    def long_step(c, _):
        rows = rows_of(c, crow)
        dq, dk, dv = softmax_grads(
            k_ref[:long_cells].reshape(flat), v_ref[:long_cells].reshape(flat),
            q_ref[rows, :], g_ref[rows, :],
            long_key <= long_query + c * cell, scale,
        )
        dq_ref[rows, :] = dq.astype(BF16)
        own[0, :long_cells] += dk.reshape(long_cells, cell, -1)
        own[1, :long_cells] += dv.reshape(long_cells, cell, -1)
        return 0

    lax.fori_loop(0, long_cells, long_step, 0)

    def hub(r, last):
        @pl.when(r != me)
        def _():
            arrived(0, out1, in1, r)

        out2[r] = last.astype(BF16)

        @pl.when(r != me)
        def _():
            hop(1, out2, in2, r, me).start()

        block = in1[r].astype(F32)
        return jnp.where(block[0:1, :] > 0.0, block, last)

    lax.fori_loop(0, n, hub, jnp.zeros((cell, k_ref.shape[-1]), F32))
    in2[me] = out2[me]

    def take2(k, _):
        arrived(1, out2, in2, lax.rem(me + k, n))
        return 0

    lax.fori_loop(1, n, take2, 0)

    def gather(c, _):
        pos = jnp.maximum(info[c], 0)
        prev[core, c] = in2[pos]
        return 0

    lax.fori_loop(0, cells, gather, 0)
    swap_prev = swap(0, prev.at[core], prev.at[core])
    swap_prev.start()
    swap_prev.wait()

    win_key = lax.broadcasted_iota(jnp.int32, (2 * cell, crow), 0)
    win_query = lax.broadcasted_iota(jnp.int32, (2 * cell, crow), 1) // heads
    causal = win_key <= win_query + cell

    def stream_step(c, _):
        qrows = rows_of(c, crow)
        prev_key = prev[0, c]
        keys = jnp.concatenate([prev_key, k_ref[c]], axis=0)
        vals = jnp.concatenate([prev[1, c], v_ref[c]], axis=0)
        mark = prev_key.astype(F32)[0:1, :]
        mark = jnp.concatenate([mark] * (crow // mark.shape[1]), axis=1)
        bound = info[BND + c]
        start = jnp.where(mark > 0.0, mark.astype(jnp.int32), cell)
        low = jnp.where(win_query[0:1, :] < bound, start, bound + cell)
        mask = (win_key >= low) & causal
        dq, dk, dv = softmax_grads(keys, vals, q_ref[qrows, :], g_ref[qrows, :], mask, scale)
        kept = info[c] < 0
        dq_ref[qrows, :] = jnp.where(kept, dq_ref[qrows, :].astype(F32), dq).astype(BF16)
        own[0, c] = jnp.where(kept, own[0, c], dk[cell:])
        own[1, c] = jnp.where(kept, own[1, c], dv[cell:])
        dprev[0, c] = dk[:cell].astype(BF16)
        dprev[1, c] = dv[:cell].astype(BF16)
        return 0

    lax.fori_loop(0, cells, stream_step, 0)

    swap_dprev = swap(1, dprev.at[sib], dprev_rx)
    swap_dprev.start()
    swap_own = swap(2, own.at[sib], own_rx)
    swap_own.start()
    swap_dprev.wait()

    def add(c, _):
        dprev[core, c] = (dprev[core, c].astype(F32) + dprev_rx[c].astype(F32)).astype(BF16)
        return 0

    lax.fori_loop(0, cells, add, 0)

    def fill3(k, _):
        d = lax.rem(me + k, n)
        pos = jnp.maximum(info[INV + d], 0)
        out3[d] = dprev[core, pos]

        @pl.when(k != 0)
        def _():
            hop(2, out3, in3, d, me).start()

        return 0

    lax.fori_loop(0, n, fill3, 0)
    in3[me] = out3[me]

    def hub_back(k, later):
        r = n - 1 - k

        @pl.when(r != me)
        def _():
            arrived(2, out3, in3, r)

        out4[r] = later.astype(BF16)

        @pl.when(r != me)
        def _():
            hop(3, out4, in4, r, me).start()

        marks = in1[r].astype(F32)
        block = in3[r].astype(F32)
        return jnp.where(marks[0:1, :] > 0.0, block, later)

    lax.fori_loop(0, n, hub_back, jnp.zeros((cell, k_ref.shape[-1]), F32))
    in4[me] = out4[me]

    def take4(k, _):
        arrived(3, out4, in4, lax.rem(me + k, n))
        return 0

    lax.fori_loop(1, n, take4, 0)
    swap_own.wait()

    def finish(c, _):
        plan = info[c]
        back = in4[jnp.maximum(plan, 0)].astype(F32)
        total = own[core, c] + own_rx[c] + jnp.where(plan >= 0, back, 0.0)
        dkv_ref[core, c] = total.astype(BF16)
        return 0

    lax.fori_loop(0, cells, finish, 0)
    swap_out = swap(3, dkv_ref.at[core], dkv_ref.at[core])
    swap_out.start()
    sent(0, out1, in1)
    sent(1, out2, in2)
    sent(2, out3, in3)
    sent(3, out4, in4)
    swap_out.wait()


def on_device(n, query_heads, key_heads, value_heads, attend_grad, doc_ids, cell_plan):
    tokens, _, heads, width = query_heads.shape
    cells = cell_plan.shape[0]
    cell = tokens // cells
    doc = doc_ids.reshape(cells, cell)
    bound = jnp.sum((doc == doc[:, :1]).astype(jnp.int32), axis=1)
    match = cell_plan[None, :] == jnp.arange(n, dtype=jnp.int32)[:, None]
    inverse = jnp.sum(jnp.where(match, jnp.arange(cells, dtype=jnp.int32)[None, :] + 1, 0), axis=1) - 1
    info = jnp.concatenate([cell_plan, inverse, bound])

    slots = pltpu.VMEM((n, cell, width), BF16)
    vmem = pl.BlockSpec(memory_space=pltpu.VMEM)
    dq, dkv = pl.pallas_call(
        functools.partial(kernel, n, cells, cell, LONG, heads),
        out_shape=(
            jax.ShapeDtypeStruct((tokens * heads, width), BF16),
            jax.ShapeDtypeStruct((2, cells, cell, width), BF16),
        ),
        in_specs=[pl.BlockSpec(memory_space=pltpu.SMEM)] + [vmem] * 4,
        out_specs=(vmem, vmem),
        scratch_shapes=[slots] * 8
        + [
            pltpu.VMEM((2, cells, cell, width), BF16),
            pltpu.VMEM((2, cells, cell, width), BF16),
            pltpu.VMEM((cells, cell, width), BF16),
            pltpu.VMEM((2, cells, cell, width), F32),
            pltpu.VMEM((cells, cell, width), F32),
            pltpu.SemaphoreType.DMA((4, n)),
            pltpu.SemaphoreType.DMA((4, n)),
            pltpu.SemaphoreType.DMA((4,)),
            pltpu.SemaphoreType.DMA((4,)),
        ],
        compiler_params=pltpu.CompilerParams(
            collective_id=0, has_side_effects=True, vmem_limit_bytes=48 * 2**20
        ),
    )(
        info,
        query_heads.reshape(tokens * heads, width),
        key_heads.reshape(cells, cell, width),
        value_heads.reshape(cells, cell, width),
        attend_grad.reshape(tokens * heads, width),
    )
    return (
        dq.reshape(tokens, 1, heads, width),
        dkv[0].reshape(tokens, 1, width),
        dkv[1].reshape(tokens, 1, width),
    )


def solution(mesh):
    wide = P("dp", "tensor", "section", None)
    narrow = P("dp", "tensor", None)
    return jax.shard_map(
        functools.partial(on_device, mesh.shape["dp"]),
        mesh=mesh,
        in_specs=(wide, narrow, narrow, wide, P("dp"), P("dp")),
        out_specs=(wide, narrow, narrow),
        check_vma=False,
    )
```

profile of v0, /device:TPU:1, one launch (start us, length us, event | category | flops | bytes accessed | tf_op | source)
XLA Modules:
  0.0 91.0 jit_solution(12760197265626939819)
XLA Ops:
  0.6 0.0 copy-start.5
  0.6 0.0 copy-start.4
  0.7 0.6 copy-done.5
  1.3 0.1 select_reduce_fusion
  1.4 0.0 copy-done.4
  1.4 0.1 reshape.30
  1.5 0.1 slice_reduce_fusion
  1.6 0.2 convert_reduce_fusion
  1.8 0.1 pad_add_fusion.info
  1.8 0.0 copy-start
  1.8 1.2 %copy-done = bf16[1024,1,4,128]{3,2,1,0:T(4,128)(2,1)S(1)} copy-done((bf16[1024,1,4,128]{3,2,1,0:T(4,128)(2,1)S(1)}, bf16[1024,1,4,128]{3,2,1,0:T(4,128)(2,1)}, u32[]{:S(2)}) %copy-start) | copy-done | bytes 1048600
  3.1 0.0 copy-start.1
  3.1 1.2 %copy-done.1 = bf16[1024,1,4,128]{3,2,1,0:T(4,128)(2,1)S(1)} copy-done((bf16[1024,1,4,128]{3,2,1,0:T(4,128)(2,1)S(1)}, bf16[1024,1,4,128]{3,2,1,0:T(4,128)(2,1)}, u32[]{:S(2)}) %copy-start.1) | copy-done | bytes 1048600
  4.3 0.0 copy-start.2
  4.3 0.9 %copy-done.2 = bf16[1024,1,128]{2,0,1:T(8,128)(2,1)S(1)} copy-done((bf16[1024,1,128]{2,0,1:T(8,128)(2,1)S(1)}, bf16[1024,1,128]{2,0,1:T(8,128)(2,1)}, u32[]{:S(2)}) %copy-start.2) | copy-done | bytes 262168
  5.2 0.0 copy-start.3
  5.3 0.9 %copy-done.3 = bf16[1024,1,128]{2,0,1:T(8,128)(2,1)S(1)} copy-done((bf16[1024,1,128]{2,0,1:T(8,128)(2,1)S(1)}, bf16[1024,1,128]{2,0,1:T(8,128)(2,1)}, u32[]{:S(2)}) %copy-start.3) | copy-done | bytes 262168
  6.2 83.0 %shard_map.85 = (bf16[4096,128]{1,0:T(8,128)(2,1)S(1)}, bf16[2,16,64,128]{3,2,1,0:T(8,128)(2,1)S(1)}) custom-call(s32[64]{0:T(128)S(1)} %pad_add_fusion.info, bf16[4096,128]{1,0:T(8,128)(2,1)S(1)} %bitcast.9, bf16[16,64,128]{2,1,0:T(8,128)(2,1)S(1)} %bitcast.12, bf16[16,64,128]{2,1,0:T(8,128)(2,1)S(1)} %bitcast.13, bf16[4096,128]{1,0:T(8,128)(2,1)S(1)} %bitcast.10), custom_call_target="tpu_custom_call" | custom-call | tf_op jit(solution)/shard_map/pallas_call | solution.py:283
  89.2 0.8 fusion
  90.0 1.0 %copy.14 = bf16[1024,1,4,128]{3,2,1,0:T(4,128)(2,1)} copy(bf16[1024,1,4,128]{3,2,1,0:T(4,128)(2,1)S(1)} %bitcast.11) | data formatting | bytes 2097152
  (2 shorter events, 0.0 us)
Async XLA Ops:
  0.6 0.7 copy-start.5
  0.6 0.7 copy-start.4
  1.8 1.2 %copy-start = (bf16[1024,1,4,128]{3,2,1,0:T(4,128)(2,1)S(1)}, bf16[1024,1,4,128]{3,2,1,0:T(4,128)(2,1)}, u32[]{:S(2)}) copy-start(bf16[1024,1,4,128]{3,2,1,0:T(4,128)(2,1)} %param.6) | copy-start | bytes 3145732
  3.1 1.2 %copy-start.1 = (bf16[1024,1,4,128]{3,2,1,0:T(4,128)(2,1)S(1)}, bf16[1024,1,4,128]{3,2,1,0:T(4,128)(2,1)}, u32[]{:S(2)}) copy-start(bf16[1024,1,4,128]{3,2,1,0:T(4,128)(2,1)} %param.9) | copy-start | bytes 3145732
  4.3 0.9 %copy-start.2 = (bf16[1024,1,128]{2,0,1:T(8,128)(2,1)S(1)}, bf16[1024,1,128]{2,0,1:T(8,128)(2,1)}, u32[]{:S(2)}) copy-start(bf16[1024,1,128]{2,0,1:T(8,128)(2,1)} %param.7) | copy-start | bytes 786436
  5.2 0.9 %copy-start.3 = (bf16[1024,1,128]{2,0,1:T(8,128)(2,1)S(1)}, bf16[1024,1,128]{2,0,1:T(8,128)(2,1)}, u32[]{:S(2)}) copy-start(bf16[1024,1,128]{2,0,1:T(8,128)(2,1)} %param.8) | copy-start | bytes 786436
where the time goes:
time: 91.2 us; the launch traced here: 91 us
  Pallas kernels  83 us (91%)
  local copies, waits for them, and re-layouts  6.97 us (8%)
    pallas_call x1, Pallas kernels, on_device(): pl.pallas_call(functools.partial(kernel, n, cells, cell, LONG, heads), ou...  83 us
    unnamed x13, local copies, waits for them, and re-layouts  5.96 us

commit v1 on v0

v1 whole, which is shorter than its diff:
```python
import functools

import jax
import jax.numpy as jnp
from jax import lax
from jax.experimental import pallas as pl
from jax.experimental.pallas import tpu as pltpu
from jax.sharding import PartitionSpec as P

LONG = 8
CHUNKS = 4
MESH = pl.DeviceIdType.MESH
LOG2E = 1.4426950408889634
NEG = -1e30
F32 = jnp.float32
BF16 = jnp.bfloat16
NT = (((1,), (1,)), ((), ()))
TN = (((0,), (0,)), ((), ()))


def rows_of(index, count):
    return pl.ds(pl.multiple_of(index * count, count), count)


def dot(a, b, dims=(((1,), (0,)), ((), ()))):
    return lax.dot_general(a, b, dims, preferred_element_type=F32)


def softmax_grads(keys, vals, quer, grad, mask, scale):
    scores = jnp.where(mask, dot(keys, quer, NT), NEG)
    prob_grad = dot(vals, grad, NT)
    top = jnp.max(scores, axis=0, keepdims=True)
    unnorm = jnp.exp2((scores - top) * (scale * LOG2E))
    probs = unnorm * (1.0 / jnp.sum(unnorm, axis=0, keepdims=True))
    delta = jnp.sum(probs * prob_grad, axis=0, keepdims=True)
    dscore = (probs * (prob_grad - delta)).astype(BF16)
    dv = dot(probs.astype(BF16), grad)
    dk = dot(dscore, quer) * scale
    dq = dot(dscore, keys, TN) * scale
    return dq, dk, dv


def kernel(
    n, cells, cell, long_cells, heads,
    plan_hbm, doc_hbm, q_hbm, k_hbm, v_hbm, g_hbm,
    dq_ref, dkv_ref,
    plan, doc, inverse, bound, q_ref, k_ref, v_ref, g_ref,
    in1, out1, in2, out2, in3, out3, in4, out4,
    prev, dprev, dprev_rx, own, own_rx, stats, dscore_prev,
    load_sem, send_sem, slot_sem, all_sem, sib_send, sib_recv,
):
    me = lax.axis_index("dp")
    core = lax.axis_index("section")
    sib = 1 - core
    crow = cell * heads
    width = q_ref.shape[-1]
    scale = width ** -0.5
    chunk = cells // CHUNKS

    loads = [
        pltpu.make_async_copy(src, dst, load_sem.at[i])
        for i, (src, dst) in enumerate(
            ((plan_hbm, plan), (doc_hbm, doc), (k_hbm, k_ref), (v_hbm, v_ref), (q_hbm, q_ref), (g_hbm, g_ref))
        )
    ]
    for load in loads:
        load.start()

    barrier = pltpu.get_barrier_semaphore()

    def greet(k, _):
        pl.semaphore_signal(
            barrier, inc=1, device_id={"dp": lax.rem(me + k, n)}, device_id_type=MESH
        )
        return 0

    lax.fori_loop(1, n, greet, 0)
    pl.semaphore_signal(barrier, inc=1, device_id={"section": sib}, device_id_type=MESH)

    def hop(phase, src, dst, peer, slot, recv):
        return pltpu.make_async_remote_copy(
            src_ref=src.at[peer],
            dst_ref=dst.at[slot],
            send_sem=send_sem.at[phase],
            recv_sem=recv,
            device_id={"dp": peer},
            device_id_type=MESH,
        )

    def whole(phase, src, dst):
        return pltpu.make_async_remote_copy(
            src_ref=src.at[pl.ds(0, n - 1)],
            dst_ref=dst.at[pl.ds(0, n - 1)],
            send_sem=send_sem.at[phase],
            recv_sem=all_sem.at[phase],
            device_id={"section": sib},
            device_id_type=MESH,
        )

    def swap(which, src, dst):
        return pltpu.make_async_remote_copy(
            src_ref=src,
            dst_ref=dst,
            send_sem=sib_send.at[which],
            recv_sem=sib_recv.at[which],
            device_id={"section": sib},
            device_id_type=MESH,
        )

    loads[0].wait()
    loads[1].wait()

    def bounds(c, _):
        base = c * cell
        lead = doc[base]
        last = jnp.int32(0)
        step = cell // 2
        while step:
            last = jnp.where(doc[base + last + step] == lead, last + step, last)
            step //= 2
        bound[c] = last + 1
        return 0

    lax.fori_loop(0, cells, bounds, 0, unroll=4)

    def invert(d, _):
        at = jnp.int32(-1)
        for c in range(cells):
            at = jnp.where(plan[c] == d, c, at)
        inverse[d] = at
        return 0

    lax.fori_loop(0, n, invert, 0, unroll=2)

    loads[2].wait()
    loads[3].wait()
    first_row = lax.broadcasted_iota(jnp.int32, (cell, width), 0) == 0

    def fill(d, _):
        at = inverse[d]
        pos = jnp.maximum(at, 0)
        block = jnp.where(core == 0, k_ref[pos], v_ref[pos]).astype(F32)
        block = jnp.where(first_row, bound[pos].astype(F32), block)
        out1[d] = jnp.where(at >= 0, block, 0.0).astype(BF16)
        return 0

    lax.fori_loop(0, n, fill, 0, unroll=4)
    in1[me] = out1[me]

    pl.semaphore_wait(barrier, n)

    def launch1(k, _):
        hop(0, out1, in1, lax.rem(me + k, n), me, slot_sem.at[0, me]).start()
        return 0

    lax.fori_loop(1, n, launch1, 0)

    loads[4].wait()
    loads[5].wait()
    long_len = long_cells * cell
    own[...] = jnp.zeros(own.shape, F32)
    dq_ref[long_cells * crow :, :] = jnp.zeros(
        (dq_ref.shape[0] - long_cells * crow, dq_ref.shape[1]), BF16
    )
    flat = (long_len, width)
    long_key = lax.broadcasted_iota(jnp.int32, (long_len, crow), 0)
    long_query = lax.broadcasted_iota(jnp.int32, (long_len, crow), 1) // heads

    def long_step(c, _):
        rows = rows_of(c, crow)
        dq, dk, dv = softmax_grads(
            k_ref[:long_cells].reshape(flat), v_ref[:long_cells].reshape(flat),
            q_ref[rows, :], g_ref[rows, :],
            long_key <= long_query + c * cell, scale,
        )
        dq_ref[rows, :] = dq.astype(BF16)
        own[0, :long_cells] += dk.reshape(long_cells, cell, -1)
        own[1, :long_cells] += dv.reshape(long_cells, cell, -1)
        return 0

    lax.fori_loop(0, long_cells, long_step, 0)

    def hub(r, last):
        @pl.when(r != me)
        def _():
            hop(0, out1, in1, r, r, slot_sem.at[0, r]).wait_recv()

        out2[r] = last.astype(BF16)

        @pl.when(r != me)
        def _():
            hop(1, out2, in2, r, me, all_sem.at[1]).start()

        block = in1[r].astype(F32)
        return jnp.where(block[0:1, :] > 0.0, block, last)

    lax.fori_loop(0, n, hub, jnp.zeros((cell, width), F32))
    in2[me] = out2[me]
    whole(0, out1, in1).wait_send()

    key_at = lax.broadcasted_iota(jnp.int32, (cell, crow), 0)
    query_at = lax.broadcasted_iota(jnp.int32, (cell, crow), 1) // heads
    causal = key_at <= query_at
    query_row = query_at[0:1, :]

    def own_block(c):
        rows = rows_of(c, crow)
        low = jnp.where(query_row < bound[c], 0, bound[c])
        scores = jnp.where(causal & (key_at >= low), dot(k_ref[c], q_ref[rows, :], NT), NEG)
        return scores, dot(v_ref[c], g_ref[rows, :], NT)

    def own_stats(c, _):
        scores, prob_grad = own_block(c)
        top = jnp.max(scores, axis=0, keepdims=True)
        unnorm = jnp.exp2((scores - top) * (scale * LOG2E))
        stats[c, 0:1] = top
        stats[c, 1:2] = jnp.sum(unnorm, axis=0, keepdims=True)
        stats[c, 2:3] = jnp.sum(unnorm * prob_grad, axis=0, keepdims=True)
        return 0

    lax.fori_loop(0, cells, own_stats, 0, unroll=4)

    whole(1, out2, in2).wait_recv()
    swaps = []
    for part in range(CHUNKS):
        span = pl.ds(part * chunk, chunk)
        for c in range(part * chunk, (part + 1) * chunk):
            prev[core, c] = in2[jnp.maximum(plan[c], 0)]
        swaps.append(swap(part, prev.at[core, span], prev.at[core, span]))
        swaps[-1].start()

    def cross(c, _):
        rows = rows_of(c, crow)
        quer, grad = q_ref[rows, :], g_ref[rows, :]
        prev_key = prev[0, c]
        mark = prev_key.astype(F32)[0:1, :]
        mark = jnp.concatenate([mark] * (crow // width), axis=1)
        mark = jnp.where(mark > 0.0, mark.astype(jnp.int32), cell)
        low = jnp.where(query_row < bound[c], mark, cell)
        scores = jnp.where(key_at >= low, dot(prev_key, quer, NT), NEG)
        prob_grad = dot(prev[1, c], grad, NT)
        own_top = stats[c, 0:1]
        top = jnp.maximum(jnp.max(scores, axis=0, keepdims=True), own_top)
        unnorm = jnp.exp2((scores - top) * (scale * LOG2E))
        shrink = jnp.exp2((own_top - top) * (scale * LOG2E))
        inv = 1.0 / (jnp.sum(unnorm, axis=0, keepdims=True) + shrink * stats[c, 1:2])
        delta = inv * (
            jnp.sum(unnorm * prob_grad, axis=0, keepdims=True) + shrink * stats[c, 2:3]
        )
        probs = unnorm * inv
        dscore = (probs * (prob_grad - delta)).astype(BF16)
        stats[c, 0:1] = top
        stats[c, 1:2] = inv
        stats[c, 2:3] = delta
        dscore_prev[c] = dscore
        dprev[0, c] = (dot(dscore, quer) * scale).astype(BF16)
        dprev[1, c] = dot(probs.astype(BF16), grad).astype(BF16)
        return 0

    back = []
    for part in range(CHUNKS):
        span = pl.ds(part * chunk, chunk)
        swaps[part].wait_recv()
        lax.fori_loop(part * chunk, (part + 1) * chunk, cross, 0, unroll=True)
        back.append(swap(CHUNKS + part, dprev.at[sib, span], dprev_rx.at[span]))
        back[-1].start()
    for part in range(CHUNKS):
        back[part].wait_recv()

    def fill3(k, _):
        d = lax.rem(me + k, n)
        pos = jnp.maximum(inverse[d], 0)
        out3[d] = (dprev[core, pos].astype(F32) + dprev_rx[pos].astype(F32)).astype(BF16)

        @pl.when(k != 0)
        def _():
            hop(2, out3, in3, d, me, slot_sem.at[1, me]).start()

        return 0

    lax.fori_loop(0, n, fill3, 0)
    in3[me] = out3[me]
    whole(1, out2, in2).wait_send()

    def own_grads(c, _):
        rows = rows_of(c, crow)
        quer, grad = q_ref[rows, :], g_ref[rows, :]
        scores, prob_grad = own_block(c)
        probs = jnp.exp2((scores - stats[c, 0:1]) * (scale * LOG2E)) * stats[c, 1:2]
        dscore = (probs * (prob_grad - stats[c, 2:3])).astype(BF16)
        dv = dot(probs.astype(BF16), grad)
        dk = dot(dscore, quer) * scale
        dq = (dot(dscore, k_ref[c], TN) + dot(dscore_prev[c], prev[0, c], TN)) * scale
        kept = plan[c] < 0
        dq_ref[rows, :] = jnp.where(kept, dq_ref[rows, :].astype(F32), dq).astype(BF16)
        own[0, c] = jnp.where(kept, own[0, c], dk)
        own[1, c] = jnp.where(kept, own[1, c], dv)
        return 0

    lax.fori_loop(0, cells, own_grads, 0, unroll=2)
    swap_own = swap(2 * CHUNKS, own.at[sib], own_rx)
    swap_own.start()

    def hub_back(k, later):
        r = n - 1 - k

        @pl.when(r != me)
        def _():
            hop(2, out3, in3, r, r, slot_sem.at[1, r]).wait_recv()

        out4[r] = later.astype(BF16)

        @pl.when(r != me)
        def _():
            hop(3, out4, in4, r, me, all_sem.at[3]).start()

        marks = in1[r].astype(F32)
        return jnp.where(marks[0:1, :] > 0.0, in3[r].astype(F32), later)

    lax.fori_loop(0, n, hub_back, jnp.zeros((cell, width), F32))
    in4[me] = out4[me]
    whole(2, out3, in3).wait_send()
    for part in range(CHUNKS):
        swaps[part].wait_send()
        back[part].wait_send()
    swap_own.wait()
    whole(3, out4, in4).wait_recv()

    last = []
    for part in range(CHUNKS):
        span = pl.ds(part * chunk, chunk)
        for c in range(part * chunk, (part + 1) * chunk):
            home = plan[c]
            came = in4[jnp.maximum(home, 0)].astype(F32)
            total = own[core, c] + own_rx[c] + jnp.where(home >= 0, came, 0.0)
            dkv_ref[core, c] = total.astype(BF16)
        last.append(swap(2 * CHUNKS + 1 + part, dkv_ref.at[core, span], dkv_ref.at[core, span]))
        last[-1].start()
    whole(3, out4, in4).wait_send()
    for part in range(CHUNKS):
        last[part].wait()


def on_device(n, query_heads, key_heads, value_heads, attend_grad, doc_ids, cell_plan):
    tokens, _, heads, width = query_heads.shape
    cells = cell_plan.shape[0]
    cell = tokens // cells
    crow = cell * heads

    slots = pltpu.VMEM((n, cell, width), BF16)
    pair = pltpu.VMEM((2, cells, cell, width), BF16)
    vmem = pl.BlockSpec(memory_space=pltpu.VMEM)
    hbm = pl.BlockSpec(memory_space=pl.ANY)
    wide = pltpu.VMEM((tokens * heads, width), BF16)
    narrow = pltpu.VMEM((cells, cell, width), BF16)
    n_swaps = 3 * CHUNKS + 1
    dq, dkv = pl.pallas_call(
        functools.partial(kernel, n, cells, cell, LONG, heads),
        out_shape=(
            jax.ShapeDtypeStruct((tokens * heads, width), BF16),
            jax.ShapeDtypeStruct((2, cells, cell, width), BF16),
        ),
        in_specs=[hbm] * 6,
        out_specs=(vmem, vmem),
        scratch_shapes=[
            pltpu.SMEM((cells,), jnp.int32),
            pltpu.SMEM((tokens,), jnp.int32),
            pltpu.SMEM((n,), jnp.int32),
            pltpu.SMEM((cells,), jnp.int32),
            wide, narrow, narrow, wide,
        ]
        + [slots] * 8
        + [
            pair, pair, narrow,
            pltpu.VMEM((2, cells, cell, width), F32),
            pltpu.VMEM((cells, cell, width), F32),
            pltpu.VMEM((cells, 8, crow), F32),
            pltpu.VMEM((cells, cell, crow), BF16),
            pltpu.SemaphoreType.DMA((6,)),
            pltpu.SemaphoreType.DMA((4,)),
            pltpu.SemaphoreType.DMA((2, n)),
            pltpu.SemaphoreType.DMA((4,)),
            pltpu.SemaphoreType.DMA((n_swaps,)),
            pltpu.SemaphoreType.DMA((n_swaps,)),
        ],
        compiler_params=pltpu.CompilerParams(
            collective_id=0, has_side_effects=True, vmem_limit_bytes=48 * 2**20
        ),
    )(
        cell_plan,
        doc_ids,
        query_heads.reshape(tokens * heads, width),
        key_heads.reshape(cells, cell, width),
        value_heads.reshape(cells, cell, width),
        attend_grad.reshape(tokens * heads, width),
    )
    return (
        dq.reshape(tokens, 1, heads, width),
        dkv[0].reshape(tokens, 1, width),
        dkv[1].reshape(tokens, 1, width),
    )


def solution(mesh):
    wide = P("dp", "tensor", "section", None)
    narrow = P("dp", "tensor", None)
    return jax.shard_map(
        functools.partial(on_device, mesh.shape["dp"]),
        mesh=mesh,
        in_specs=(wide, narrow, narrow, wide, P("dp"), P("dp")),
        out_specs=(wide, narrow, narrow),
        check_vma=False,
    )
```

time: 91.2 us -> 83 us (0.910)
  Pallas kernels: 83 us -> 75.3 us
    pallas_call x1, Pallas kernels: 83 us -> 75.3 us  [on_device(): pl.pallas_call(functools.partial(kernel, n, cells, cell, LONG, heads), ou...]
where the time goes in v1:
time: 83 us; the launch traced here: 82.8 us
  Pallas kernels  75.3 us (91%)
  local copies, waits for them, and re-layouts  6.82 us (8%)
    pallas_call x1, Pallas kernels, on_device(): pl.pallas_call(functools.partial(kernel, n, cells, cell, LONG, heads), ou...  75.3 us
    unnamed x13, local copies, waits for them, and re-layouts  5.99 us

profile of v1, /device:TPU:1, one launch (start us, length us, event | category | flops | bytes accessed | tf_op | source)
XLA Modules:
  0.0 82.8 jit_solution(11566604161861409644)
XLA Ops:
  0.6 0.0 copy-start.4
  0.6 0.0 copy-start.5
  0.7 0.7 copy-done.4
  1.3 0.0 copy-done.5
  1.3 0.0 copy-start
  1.3 1.2 %copy-done = bf16[1024,1,4,128]{3,2,1,0:T(4,128)(2,1)S(1)} copy-done((bf16[1024,1,4,128]{3,2,1,0:T(4,128)(2,1)S(1)}, bf16[1024,1,4,128]{3,2,1,0:T(4,128)(2,1)}, u32[]{:S(2)}) %copy-start) | copy-done | bytes 1048600
  2.5 0.0 copy-start.1
  2.6 1.2 %copy-done.1 = bf16[1024,1,4,128]{3,2,1,0:T(4,128)(2,1)S(1)} copy-done((bf16[1024,1,4,128]{3,2,1,0:T(4,128)(2,1)S(1)}, bf16[1024,1,4,128]{3,2,1,0:T(4,128)(2,1)}, u32[]{:S(2)}) %copy-start.1) | copy-done | bytes 1048600
  3.8 0.0 copy-start.2
  3.8 0.9 %copy-done.2 = bf16[1024,1,128]{2,0,1:T(8,128)(2,1)S(1)} copy-done((bf16[1024,1,128]{2,0,1:T(8,128)(2,1)S(1)}, bf16[1024,1,128]{2,0,1:T(8,128)(2,1)}, u32[]{:S(2)}) %copy-start.2) | copy-done | bytes 262168
  4.7 0.0 copy-start.3
  4.7 0.9 %copy-done.3 = bf16[1024,1,128]{2,0,1:T(8,128)(2,1)S(1)} copy-done((bf16[1024,1,128]{2,0,1:T(8,128)(2,1)S(1)}, bf16[1024,1,128]{2,0,1:T(8,128)(2,1)}, u32[]{:S(2)}) %copy-start.3) | copy-done | bytes 262168
  5.7 75.3 %shard_map.85 = (bf16[4096,128]{1,0:T(8,128)(2,1)S(1)}, bf16[2,16,64,128]{3,2,1,0:T(8,128)(2,1)S(1)}) custom-call(s32[16]{0:T(128)S(1)} %copy-done.5, s32[1024]{0:T(1024)S(1)} %copy-done.4, bf16[4096,128]{1,0:T(8,128)(2,1)S(1)} %bitcast.9, bf16[16,64,128]{2,1,0:T(8,128)(2,1)S(1)} %bitcast.12, bf16[16,64,128]{2,1,0:T(8,128)(2,1)S(1)} %bitcast.13, ...), custom_call_target="tpu_custom_call" | custom-call | tf_op jit(solution)/shard_map/pallas_call | solution.py:357
  81.0 0.8 fusion
  81.8 1.0 %copy.11 = bf16[1024,1,4,128]{3,2,1,0:T(4,128)(2,1)} copy(bf16[1024,1,4,128]{3,2,1,0:T(4,128)(2,1)S(1)} %bitcast.11) | data formatting | bytes 2097152
Async XLA Ops:
  0.6 0.7 copy-start.4
  0.6 0.7 copy-start.5
  1.3 1.2 %copy-start = (bf16[1024,1,4,128]{3,2,1,0:T(4,128)(2,1)S(1)}, bf16[1024,1,4,128]{3,2,1,0:T(4,128)(2,1)}, u32[]{:S(2)}) copy-start(bf16[1024,1,4,128]{3,2,1,0:T(4,128)(2,1)} %param.6) | copy-start | bytes 3145732
  2.5 1.2 %copy-start.1 = (bf16[1024,1,4,128]{3,2,1,0:T(4,128)(2,1)S(1)}, bf16[1024,1,4,128]{3,2,1,0:T(4,128)(2,1)}, u32[]{:S(2)}) copy-start(bf16[1024,1,4,128]{3,2,1,0:T(4,128)(2,1)} %param.9) | copy-start | bytes 3145732
  3.8 0.9 %copy-start.2 = (bf16[1024,1,128]{2,0,1:T(8,128)(2,1)S(1)}, bf16[1024,1,128]{2,0,1:T(8,128)(2,1)}, u32[]{:S(2)}) copy-start(bf16[1024,1,128]{2,0,1:T(8,128)(2,1)} %param.7) | copy-start | bytes 786436
  4.7 0.9 %copy-start.3 = (bf16[1024,1,128]{2,0,1:T(8,128)(2,1)S(1)}, bf16[1024,1,128]{2,0,1:T(8,128)(2,1)}, u32[]{:S(2)}) copy-start(bf16[1024,1,128]{2,0,1:T(8,128)(2,1)} %param.8) | copy-start | bytes 786436

commit v2 on v1

--- a/solution.py
+++ b/solution.py
@@ -9,6 +9,7 @@
 
 LONG = 8
 CHUNKS = 4
+PARTS = 4
 MESH = pl.DeviceIdType.MESH
 LOG2E = 1.4426950408889634
 NEG = -1e30
@@ -43,11 +44,11 @@
 def kernel(
     n, cells, cell, long_cells, heads,
     plan_hbm, doc_hbm, q_hbm, k_hbm, v_hbm, g_hbm,
-    dq_ref, dkv_ref,
-    plan, doc, inverse, bound, q_ref, k_ref, v_ref, g_ref,
+    dq_hbm, dk_hbm, dv_hbm,
+    plan, doc, flags, rank, slot, inverse, bound, q_ref, k_ref, v_ref, g_ref, dq_ref, total_ref, marked,
     in1, out1, in2, out2, in3, out3, in4, out4,
     prev, dprev, dprev_rx, own, own_rx, stats, dscore_prev,
-    load_sem, send_sem, slot_sem, all_sem, sib_send, sib_recv,
+    load_sem, send_sem, slot_sem, all_sem, sib_send, sib_recv, store_sem,
 ):
     me = lax.axis_index("dp")
     core = lax.axis_index("section")
@@ -56,6 +57,9 @@
     width = q_ref.shape[-1]
     scale = width ** -0.5
     chunk = cells // CHUNKS
+    part_rows = cell // PARTS
+    n_slots = 3 * n // 4
+    deal = n_slots * PARTS // n
 
     loads = [
         pltpu.make_async_copy(src, dst, load_sem.at[i])
@@ -77,10 +81,10 @@
     lax.fori_loop(1, n, greet, 0)
     pl.semaphore_signal(barrier, inc=1, device_id={"section": sib}, device_id_type=MESH)
 
-    def hop(phase, src, dst, peer, slot, recv):
+    def hop(phase, src, dst, peer, place, recv):
         return pltpu.make_async_remote_copy(
-            src_ref=src.at[peer],
-            dst_ref=dst.at[slot],
+            src_ref=src.at[pl.ds(peer * deal, deal)],
+            dst_ref=dst.at[pl.ds(place * deal, deal)],
             send_sem=send_sem.at[phase],
             recv_sem=recv,
             device_id={"dp": peer},
@@ -89,8 +93,8 @@
 
     def whole(phase, src, dst):
         return pltpu.make_async_remote_copy(
-            src_ref=src.at[pl.ds(0, n - 1)],
-            dst_ref=dst.at[pl.ds(0, n - 1)],
+            src_ref=src.at[pl.ds(0, (n - 1) * deal)],
+            dst_ref=dst.at[pl.ds(0, (n - 1) * deal)],
             send_sem=send_sem.at[phase],
             recv_sem=all_sem.at[phase],
             device_id={"section": sib},
@@ -123,31 +127,70 @@
 
     lax.fori_loop(0, cells, bounds, 0, unroll=4)
 
-    def invert(d, _):
+    for i in range(flags.shape[1]):
+        flags[me, i] = plan[0]
+
+    loads[2].wait()
+    loads[3].wait()
+    row_at = lax.broadcasted_iota(jnp.int32, (cell, width), 0)
+
+    def mark(c, _):
+        block = jnp.where(core == 0, k_ref[c], v_ref[c]).astype(F32)
+        moved = block
+        for i in range(1, PARTS):
+            moved = jnp.where(row_at == i, block[i * part_rows : i * part_rows + 1, :], moved)
+        moved = jnp.where(row_at % part_rows == 0, bound[c].astype(F32), moved)
+        marked[c] = moved.astype(BF16)
+        return 0
+
+    lax.fori_loop(0, cells, mark, 0, unroll=4)
+
+    pl.semaphore_wait(barrier, n)
+
+    def tell(k, _):
+        pltpu.make_async_remote_copy(
+            src_ref=flags.at[me],
+            dst_ref=flags.at[me],
+            send_sem=send_sem.at[4],
+            recv_sem=all_sem.at[0],
+            device_id={"dp": lax.rem(me + k, n)},
+            device_id_type=MESH,
+        ).start()
+        return 0
+
+    lax.fori_loop(1, n, tell, 0)
+    told = pltpu.make_async_remote_copy(
+        src_ref=flags.at[pl.ds(0, n - 1)],
+        dst_ref=flags.at[pl.ds(0, n - 1)],
+        send_sem=send_sem.at[4],
+        recv_sem=all_sem.at[0],
+        device_id={"section": sib},
+        device_id_type=MESH,
+    )
+    told.wait_recv()
+
+    keepers = jnp.int32(0)
+    for d in range(n):
+        rank[d] = d - keepers
+        keepers += jnp.where(flags[d, 0] < 0, 1, 0)
+    for c in range(cells):
+        slot[c] = jnp.where(plan[c] >= 0, rank[jnp.maximum(plan[c], 0)], -1)
+
+    def fill(j, _):
         at = jnp.int32(-1)
         for c in range(cells):
-            at = jnp.where(plan[c] == d, c, at)
-        inverse[d] = at
-        return 0
-
-    lax.fori_loop(0, n, invert, 0, unroll=2)
-
-    loads[2].wait()
-    loads[3].wait()
-    first_row = lax.broadcasted_iota(jnp.int32, (cell, width), 0) == 0
-
-    def fill(d, _):
-        at = inverse[d]
-        pos = jnp.maximum(at, 0)
-        block = jnp.where(core == 0, k_ref[pos], v_ref[pos]).astype(F32)
-        block = jnp.where(first_row, bound[pos].astype(F32), block)
-        out1[d] = jnp.where(at >= 0, block, 0.0).astype(BF16)
-        return 0
-
-    lax.fori_loop(0, n, fill, 0, unroll=4)
-    in1[me] = out1[me]
-
-    pl.semaphore_wait(barrier, n)
+            at = jnp.where(slot[c] == j, c, at)
+        inverse[j] = at
+        block = jnp.where(at >= 0, marked[jnp.maximum(at, 0)], jnp.zeros((cell, width), BF16))
+        out1[pl.ds(j * PARTS, PARTS)] = block.reshape(PARTS, part_rows, width)
+        return 0
+
+    lax.fori_loop(0, n_slots, fill, 0, unroll=2)
+
+    def mine(ref):
+        return ref[pl.ds(me * deal, deal)]
+
+    in1[pl.ds(me * deal, deal)] = mine(out1)
 
     def launch1(k, _):
         hop(0, out1, in1, lax.rem(me + k, n), me, slot_sem.at[0, me]).start()
@@ -185,23 +228,25 @@
         def _():
             hop(0, out1, in1, r, r, slot_sem.at[0, r]).wait_recv()
 
-        out2[r] = last.astype(BF16)
+        out2[pl.ds(r * deal, deal)] = last.astype(BF16)
 
         @pl.when(r != me)
         def _():
             hop(1, out2, in2, r, me, all_sem.at[1]).start()
 
-        block = in1[r].astype(F32)
-        return jnp.where(block[0:1, :] > 0.0, block, last)
-
-    lax.fori_loop(0, n, hub, jnp.zeros((cell, width), F32))
-    in2[me] = out2[me]
+        block = in1[pl.ds(r * deal, deal)].astype(F32)
+        return jnp.where(block[:, 0:1, :] > 0.0, block, last)
+
+    lax.fori_loop(0, n, hub, jnp.zeros((deal, part_rows, width), F32))
+    in2[pl.ds(me * deal, deal)] = mine(out2)
     whole(0, out1, in1).wait_send()
 
     key_at = lax.broadcasted_iota(jnp.int32, (cell, crow), 0)
     query_at = lax.broadcasted_iota(jnp.int32, (cell, crow), 1) // heads
     causal = key_at <= query_at
     query_row = query_at[0:1, :]
+    moved_at = jnp.where(key_at < PARTS, key_at * part_rows, key_at)
+    moved_at = jnp.where(key_at % part_rows == 0, -1, moved_at)
 
     def own_block(c):
         rows = rows_of(c, crow)
@@ -225,7 +270,8 @@
     for part in range(CHUNKS):
         span = pl.ds(part * chunk, chunk)
         for c in range(part * chunk, (part + 1) * chunk):
-            prev[core, c] = in2[jnp.maximum(plan[c], 0)]
+            took = in2[pl.ds(jnp.maximum(slot[c], 0) * PARTS, PARTS)]
+            prev[core, c] = took.reshape(cell, width)
         swaps.append(swap(part, prev.at[core, span], prev.at[core, span]))
         swaps[-1].start()
 
@@ -237,7 +283,7 @@
         mark = jnp.concatenate([mark] * (crow // width), axis=1)
         mark = jnp.where(mark > 0.0, mark.astype(jnp.int32), cell)
         low = jnp.where(query_row < bound[c], mark, cell)
-        scores = jnp.where(key_at >= low, dot(prev_key, quer, NT), NEG)
+        scores = jnp.where(moved_at >= low, dot(prev_key, quer, NT), NEG)
         prob_grad = dot(prev[1, c], grad, NT)
         own_top = stats[c, 0:1]
         top = jnp.maximum(jnp.max(scores, axis=0, keepdims=True), own_top)
@@ -267,19 +313,20 @@
     for part in range(CHUNKS):
         back[part].wait_recv()
 
-    def fill3(k, _):
-        d = lax.rem(me + k, n)
-        pos = jnp.maximum(inverse[d], 0)
-        out3[d] = (dprev[core, pos].astype(F32) + dprev_rx[pos].astype(F32)).astype(BF16)
-
-        @pl.when(k != 0)
-        def _():
-            hop(2, out3, in3, d, me, slot_sem.at[1, me]).start()
-
-        return 0
-
-    lax.fori_loop(0, n, fill3, 0)
-    in3[me] = out3[me]
+    def fill3(j, _):
+        pos = jnp.maximum(inverse[j], 0)
+        block = (dprev[core, pos].astype(F32) + dprev_rx[pos].astype(F32)).astype(BF16)
+        out3[pl.ds(j * PARTS, PARTS)] = block.reshape(PARTS, part_rows, width)
+        return 0
+
+    lax.fori_loop(0, n_slots, fill3, 0, unroll=2)
+
+    def launch3(k, _):
+        hop(2, out3, in3, lax.rem(me + k, n), me, slot_sem.at[1, me]).start()
+        return 0
+
+    lax.fori_loop(1, n, launch3, 0)
+    in3[pl.ds(me * deal, deal)] = mine(out3)
     whole(1, out2, in2).wait_send()
 
     def own_grads(c, _):
@@ -298,6 +345,8 @@
         return 0
 
     lax.fori_loop(0, cells, own_grads, 0, unroll=2)
+    store_q = pltpu.make_async_copy(dq_ref, dq_hbm, store_sem.at[CHUNKS])
+    store_q.start()
     swap_own = swap(2 * CHUNKS, own.at[sib], own_rx)
     swap_own.start()
 
@@ -308,17 +357,18 @@
         def _():
             hop(2, out3, in3, r, r, slot_sem.at[1, r]).wait_recv()
 
-        out4[r] = later.astype(BF16)
+        out4[pl.ds(r * deal, deal)] = later.astype(BF16)
 
         @pl.when(r != me)
         def _():
             hop(3, out4, in4, r, me, all_sem.at[3]).start()
 
-        marks = in1[r].astype(F32)
-        return jnp.where(marks[0:1, :] > 0.0, in3[r].astype(F32), later)
-
-    lax.fori_loop(0, n, hub_back, jnp.zeros((cell, width), F32))
-    in4[me] = out4[me]
+        marks = in1[pl.ds(r * deal, deal)].astype(F32)
+        block = in3[pl.ds(r * deal, deal)].astype(F32)
+        return jnp.where(marks[:, 0:1, :] > 0.0, block, later)
+
+    lax.fori_loop(0, n, hub_back, jnp.zeros((deal, part_rows, width), F32))
+    in4[pl.ds(me * deal, deal)] = mine(out4)
     whole(2, out3, in3).wait_send()
     for part in range(CHUNKS):
         swaps[part].wait_send()
@@ -326,19 +376,41 @@
     swap_own.wait()
     whole(3, out4, in4).wait_recv()
 
-    last = []
-    for part in range(CHUNKS):
+    def give(part, where):
         span = pl.ds(part * chunk, chunk)
+        return (
+            pltpu.make_async_copy(total_ref.at[span], where.at[span], store_sem.at[part]),
+            swap(2 * CHUNKS + 1 + part, total_ref.at[span], where.at[span]),
+        )
+
+    for part in range(CHUNKS):
         for c in range(part * chunk, (part + 1) * chunk):
-            home = plan[c]
-            came = in4[jnp.maximum(home, 0)].astype(F32)
-            total = own[core, c] + own_rx[c] + jnp.where(home >= 0, came, 0.0)
-            dkv_ref[core, c] = total.astype(BF16)
-        last.append(swap(2 * CHUNKS + 1 + part, dkv_ref.at[core, span], dkv_ref.at[core, span]))
-        last[-1].start()
+            came = in4[pl.ds(jnp.maximum(slot[c], 0) * PARTS, PARTS)].astype(F32).reshape(cell, width)
+            back_rows = jnp.where(row_at < PARTS, 0.0, came)
+            for i in range(1, PARTS):
+                back_rows = jnp.where(row_at == i * part_rows, came[i : i + 1, :], back_rows)
+            total = own[core, c] + own_rx[c] + jnp.where(slot[c] >= 0, back_rows, 0.0)
+            total_ref[c] = total.astype(BF16)
+
+        for which, where in ((0, dk_hbm), (1, dv_hbm)):
+
+            @pl.when(core == which)
+            def _():
+                for copy in give(part, where):
+                    copy.start()
+
     whole(3, out4, in4).wait_send()
-    for part in range(CHUNKS):
-        last[part].wait()
+    told.wait_send()
+    store_q.wait()
+    for part in range(CHUNKS):
+        for which, where, other in ((0, dk_hbm, dv_hbm), (1, dv_hbm, dk_hbm)):
+
+            @pl.when(core == which)
+            def _():
+                here, there = give(part, where)
+                here.wait()
+                there.wait_send()
+                give(part, other)[1].wait_recv()
 
 
 def on_device(n, query_heads, key_heads, value_heads, attend_grad, doc_ids, cell_plan):
@@ -347,27 +419,31 @@
     cell = tokens // cells
     crow = cell * heads
 
-    slots = pltpu.VMEM((n, cell, width), BF16)
+    n_slots = 3 * n // 4
+    slots = pltpu.VMEM((n_slots * PARTS, cell // PARTS, width), BF16)
     pair = pltpu.VMEM((2, cells, cell, width), BF16)
-    vmem = pl.BlockSpec(memory_space=pltpu.VMEM)
     hbm = pl.BlockSpec(memory_space=pl.ANY)
     wide = pltpu.VMEM((tokens * heads, width), BF16)
     narrow = pltpu.VMEM((cells, cell, width), BF16)
     n_swaps = 3 * CHUNKS + 1
-    dq, dkv = pl.pallas_call(
+    dq, dk, dv = pl.pallas_call(
         functools.partial(kernel, n, cells, cell, LONG, heads),
         out_shape=(
             jax.ShapeDtypeStruct((tokens * heads, width), BF16),
-            jax.ShapeDtypeStruct((2, cells, cell, width), BF16),
+            jax.ShapeDtypeStruct((cells, cell, width), BF16),
+            jax.ShapeDtypeStruct((cells, cell, width), BF16),
         ),
         in_specs=[hbm] * 6,
-        out_specs=(vmem, vmem),
+        out_specs=[hbm] * 3,
         scratch_shapes=[
             pltpu.SMEM((cells,), jnp.int32),
             pltpu.SMEM((tokens,), jnp.int32),
+            pltpu.SMEM((n, 8), jnp.int32),
             pltpu.SMEM((n,), jnp.int32),
             pltpu.SMEM((cells,), jnp.int32),
-            wide, narrow, narrow, wide,
+            pltpu.SMEM((n_slots,), jnp.int32),
+            pltpu.SMEM((cells,), jnp.int32),
+            wide, narrow, narrow, wide, wide, narrow, narrow,
         ]
         + [slots] * 8
         + [
@@ -377,14 +453,15 @@
             pltpu.VMEM((cells, 8, crow), F32),
             pltpu.VMEM((cells, cell, crow), BF16),
             pltpu.SemaphoreType.DMA((6,)),
-            pltpu.SemaphoreType.DMA((4,)),
+            pltpu.SemaphoreType.DMA((5,)),
             pltpu.SemaphoreType.DMA((2, n)),
             pltpu.SemaphoreType.DMA((4,)),
             pltpu.SemaphoreType.DMA((n_swaps,)),
             pltpu.SemaphoreType.DMA((n_swaps,)),
+            pltpu.SemaphoreType.DMA((CHUNKS + 1,)),
         ],
         compiler_params=pltpu.CompilerParams(
-            collective_id=0, has_side_effects=True, vmem_limit_bytes=48 * 2**20
+            collective_id=0, has_side_effects=True, vmem_limit_bytes=63 * 2**20
         ),
     )(
         cell_plan,
@@ -396,8 +473,8 @@
     )
     return (
         dq.reshape(tokens, 1, heads, width),
-        dkv[0].reshape(tokens, 1, width),
-        dkv[1].reshape(tokens, 1, width),
+        dk.reshape(tokens, 1, width),
+        dv.reshape(tokens, 1, width),
     )
 
 

time: 83 us -> 73.7 us (0.89)
  Pallas kernels: 75.3 us -> 68.5 us
  local copies, waits for them, and re-layouts: 6.82 us -> 4.35 us
    pallas_call x1, Pallas kernels: 75.3 us -> 68.5 us  [on_device(): pl.pallas_call(functools.partial(kernel, n, cells, cell, LONG, heads), ou...]
    unnamed x13 -> x7, local copies, waits for them, and re-layouts: 5.99 us -> 4.35 us
where the time goes in v2:
time: 73.7 us; the launch traced here: 73.5 us
  Pallas kernels  68.5 us (93%)
  local copies, waits for them, and re-layouts  4.35 us (6%)
    pallas_call x1, Pallas kernels, on_device(): pl.pallas_call(functools.partial(kernel, n, cells, cell, LONG, heads), ou...  68.5 us
    unnamed x7, local copies, waits for them, and re-layouts  4.35 us

profile of v2, /device:TPU:1, one launch (start us, length us, event | category | flops | bytes accessed | tf_op | source)
XLA Modules:
  0.0 73.5 jit_solution(11495310689004322578)
XLA Ops:
  0.6 68.5 %shard_map.85 = (bf16[4096,128]{1,0:T(8,128)(2,1)}, bf16[16,64,128]{2,1,0:T(8,128)(2,1)}, bf16[16,64,128]{2,1,0:T(8,128)(2,1)}) custom-call(s32[16]{0:T(128)} %plan_hbm.1, s32[1024]{0:T(1024)} %doc_hbm.1, bf16[4096,128]{1,0:T(8,128)(2,1)} %bitcast.9, bf16[16,64,128]{2,1,0:T(8,128)(2,1)} %bitcast.12, bf16[16,64,128]{2,1,0:T(8,128)(2,1)} %bitcast.13, ...), custom_call_target="tpu_custom_call" | custom-call | tf_op jit(solution)/shard_map/pallas_call | solution.py:429
  69.2 0.0 copy-start.1
  69.2 2.6 %copy.13 = bf16[1024,1,4,128]{3,2,1,0:T(4,128)(2,1)} copy(bf16[1024,1,4,128]{3,2,1,0:T(4,128)(2,1)} %bitcast.11) | data formatting | bytes 2097152
  71.8 0.0 copy-done.1
  71.8 0.0 copy-start
  71.8 0.7 copy.14
  72.5 0.3 copy-done
  72.8 0.7 copy.15
Async XLA Ops:
  69.2 2.6 %copy-start.1 = (bf16[16,64,128]{2,1,0:T(8,128)(2,1)S(1)}, bf16[16,64,128]{2,1,0:T(8,128)(2,1)}, u32[]{:S(2)}) copy-start(bf16[16,64,128]{2,1,0:T(8,128)(2,1)} %get-tuple-element.7) | copy-start | bytes 786436
  71.8 1.0 %copy-start = (bf16[16,64,128]{2,1,0:T(8,128)(2,1)S(1)}, bf16[16,64,128]{2,1,0:T(8,128)(2,1)}, u32[]{:S(2)}) copy-start(bf16[16,64,128]{2,1,0:T(8,128)(2,1)} %get-tuple-element.8) | copy-start | bytes 786436

commit v3 on v2

--- a/solution.py
+++ b/solution.py
@@ -10,6 +10,7 @@
 LONG = 8
 CHUNKS = 4
 PARTS = 4
+RING = 8
 MESH = pl.DeviceIdType.MESH
 LOG2E = 1.4426950408889634
 NEG = -1e30
@@ -44,11 +45,11 @@
 def kernel(
     n, cells, cell, long_cells, heads,
     plan_hbm, doc_hbm, q_hbm, k_hbm, v_hbm, g_hbm,
-    dq_hbm, dk_hbm, dv_hbm,
+    dq_hbm, dkv_hbm,
     plan, doc, flags, rank, slot, inverse, bound, q_ref, k_ref, v_ref, g_ref, dq_ref, total_ref, marked,
     in1, out1, in2, out2, in3, out3, in4, out4,
     prev, dprev, dprev_rx, own, own_rx, stats, dscore_prev,
-    load_sem, send_sem, slot_sem, all_sem, sib_send, sib_recv, store_sem,
+    load_sem, flag_sem, send_sem, recv_sem, sib_send, sib_recv, store_sem,
 ):
     me = lax.axis_index("dp")
     core = lax.axis_index("section")
@@ -60,6 +61,18 @@
     part_rows = cell // PARTS
     n_slots = 3 * n // 4
     deal = n_slots * PARTS // n
+    ring = min(RING, n)
+    lines = n // ring
+    line_at, ring_at = me // ring, lax.rem(me, ring)
+
+    steps = sorted(
+        ((a, b) for a in range(ring) for b in range(lines) if a or b),
+        key=lambda s: -2 * min(s[0], ring - s[0]) - min(s[1], lines - s[1]),
+    )
+
+    def peers():
+        for a, b in steps:
+            yield lax.rem(line_at + b, lines) * ring + lax.rem(ring_at + a, ring)
 
     loads = [
         pltpu.make_async_copy(src, dst, load_sem.at[i])
@@ -72,34 +85,34 @@
 
     barrier = pltpu.get_barrier_semaphore()
 
-    def greet(k, _):
-        pl.semaphore_signal(
-            barrier, inc=1, device_id={"dp": lax.rem(me + k, n)}, device_id_type=MESH
-        )
-        return 0
-
-    lax.fori_loop(1, n, greet, 0)
+    for peer in peers():
+        pl.semaphore_signal(barrier, inc=1, device_id={"dp": peer}, device_id_type=MESH)
     pl.semaphore_signal(barrier, inc=1, device_id={"section": sib}, device_id_type=MESH)
 
-    def hop(phase, src, dst, peer, place, recv):
+    def launch(phase, part, src, dst):
+        for peer in peers():
+            pltpu.make_async_remote_copy(
+                src_ref=src.at[peer * deal + part],
+                dst_ref=dst.at[me * deal + part],
+                send_sem=send_sem.at[phase, part],
+                recv_sem=recv_sem.at[phase, part],
+                device_id={"dp": peer},
+                device_id_type=MESH,
+            ).start()
+
+    def lot(phase, part, src, dst):
         return pltpu.make_async_remote_copy(
-            src_ref=src.at[pl.ds(peer * deal, deal)],
-            dst_ref=dst.at[pl.ds(place * deal, deal)],
-            send_sem=send_sem.at[phase],
-            recv_sem=recv,
-            device_id={"dp": peer},
-            device_id_type=MESH,
-        )
-
-    def whole(phase, src, dst):
-        return pltpu.make_async_remote_copy(
-            src_ref=src.at[pl.ds(0, (n - 1) * deal)],
-            dst_ref=dst.at[pl.ds(0, (n - 1) * deal)],
-            send_sem=send_sem.at[phase],
-            recv_sem=all_sem.at[phase],
+            src_ref=src.at[pl.ds(0, n - 1)],
+            dst_ref=dst.at[pl.ds(0, n - 1)],
+            send_sem=send_sem.at[phase, part],
+            recv_sem=recv_sem.at[phase, part],
             device_id={"section": sib},
             device_id_type=MESH,
         )
+
+    def sent(phase, src, dst):
+        for part in range(deal):
+            lot(phase, part, src, dst).wait_send()
 
     def swap(which, src, dst):
         return pltpu.make_async_remote_copy(
@@ -147,23 +160,20 @@
 
     pl.semaphore_wait(barrier, n)
 
-    def tell(k, _):
+    for peer in peers():
         pltpu.make_async_remote_copy(
             src_ref=flags.at[me],
             dst_ref=flags.at[me],
-            send_sem=send_sem.at[4],
-            recv_sem=all_sem.at[0],
-            device_id={"dp": lax.rem(me + k, n)},
+            send_sem=flag_sem.at[0],
+            recv_sem=flag_sem.at[1],
+            device_id={"dp": peer},
             device_id_type=MESH,
         ).start()
-        return 0
-
-    lax.fori_loop(1, n, tell, 0)
     told = pltpu.make_async_remote_copy(
         src_ref=flags.at[pl.ds(0, n - 1)],
         dst_ref=flags.at[pl.ds(0, n - 1)],
-        send_sem=send_sem.at[4],
-        recv_sem=all_sem.at[0],
+        send_sem=flag_sem.at[0],
+        recv_sem=flag_sem.at[1],
         device_id={"section": sib},
         device_id_type=MESH,
     )
@@ -192,11 +202,8 @@
 
     in1[pl.ds(me * deal, deal)] = mine(out1)
 
-    def launch1(k, _):
-        hop(0, out1, in1, lax.rem(me + k, n), me, slot_sem.at[0, me]).start()
-        return 0
-
-    lax.fori_loop(1, n, launch1, 0)
+    for part in range(deal):
+        launch(0, part, out1, in1)
 
     loads[4].wait()
     loads[5].wait()
@@ -221,25 +228,29 @@
         own[1, :long_cells] += dv.reshape(long_cells, cell, -1)
         return 0
 
-    lax.fori_loop(0, long_cells, long_step, 0)
-
-    def hub(r, last):
-        @pl.when(r != me)
-        def _():
-            hop(0, out1, in1, r, r, slot_sem.at[0, r]).wait_recv()
-
-        out2[pl.ds(r * deal, deal)] = last.astype(BF16)
-
-        @pl.when(r != me)
-        def _():
-            hop(1, out2, in2, r, me, all_sem.at[1]).start()
-
-        block = in1[pl.ds(r * deal, deal)].astype(F32)
-        return jnp.where(block[:, 0:1, :] > 0.0, block, last)
-
-    lax.fori_loop(0, n, hub, jnp.zeros((deal, part_rows, width), F32))
-    in2[pl.ds(me * deal, deal)] = mine(out2)
-    whole(0, out1, in1).wait_send()
+    def hub(part):
+        def step(r, last):
+            at = r * deal + part
+            out2[at] = last.astype(BF16)
+            block = in1[at].astype(F32)
+            return jnp.where(block[0:1, :] > 0.0, block, last)
+
+        lax.fori_loop(0, n, step, jnp.zeros((part_rows, width), F32), unroll=8)
+
+    def share(count, part):
+        return (
+            count * (deal - 2 + part) // (2 * (deal - 1)) if part else 0,
+            count * (deal - 1 + part) // (2 * (deal - 1)),
+        )
+
+    lax.fori_loop(*share(long_cells, 0), long_step, 0)
+    for part in range(deal):
+        lot(0, part, out1, in1).wait_recv()
+        hub(part)
+        launch(1, part, out2, in2)
+        in2[me * deal + part] = out2[me * deal + part]
+        if part < deal - 1:
+            lax.fori_loop(*share(long_cells, part + 1), long_step, 0)
 
     key_at = lax.broadcasted_iota(jnp.int32, (cell, crow), 0)
     query_at = lax.broadcasted_iota(jnp.int32, (cell, crow), 1) // heads
@@ -265,7 +276,9 @@
 
     lax.fori_loop(0, cells, own_stats, 0, unroll=4)
 
-    whole(1, out2, in2).wait_recv()
+    sent(0, out1, in1)
+    for part in range(deal):
+        lot(1, part, out2, in2).wait_recv()
     swaps = []
     for part in range(CHUNKS):
         span = pl.ds(part * chunk, chunk)
@@ -321,13 +334,10 @@
 
     lax.fori_loop(0, n_slots, fill3, 0, unroll=2)
 
-    def launch3(k, _):
-        hop(2, out3, in3, lax.rem(me + k, n), me, slot_sem.at[1, me]).start()
-        return 0
-
-    lax.fori_loop(1, n, launch3, 0)
+    for part in range(deal):
+        launch(2, part, out3, in3)
     in3[pl.ds(me * deal, deal)] = mine(out3)
-    whole(1, out2, in2).wait_send()
+    sent(1, out2, in2)
 
     def own_grads(c, _):
         rows = rows_of(c, crow)
@@ -344,43 +354,43 @@
         own[1, c] = jnp.where(kept, own[1, c], dv)
         return 0
 
-    lax.fori_loop(0, cells, own_grads, 0, unroll=2)
+    def hub_back(part):
+        def step(k, later):
+            at = (n - 1 - k) * deal + part
+            out4[at] = later.astype(BF16)
+            marks = in1[at].astype(F32)
+            return jnp.where(marks[0:1, :] > 0.0, in3[at].astype(F32), later)
+
+        lax.fori_loop(0, n, step, jnp.zeros((part_rows, width), F32), unroll=8)
+
+    lax.fori_loop(*share(cells, 0), own_grads, 0, unroll=2)
+    for part in range(deal):
+        lot(2, part, out3, in3).wait_recv()
+        hub_back(part)
+        launch(3, part, out4, in4)
+        in4[me * deal + part] = out4[me * deal + part]
+        if part < deal - 1:
+            lax.fori_loop(*share(cells, part + 1), own_grads, 0, unroll=2)
+    swap_own = swap(2 * CHUNKS, own.at[sib], own_rx)
+    swap_own.start()
     store_q = pltpu.make_async_copy(dq_ref, dq_hbm, store_sem.at[CHUNKS])
     store_q.start()
-    swap_own = swap(2 * CHUNKS, own.at[sib], own_rx)
-    swap_own.start()
-
-    def hub_back(k, later):
-        r = n - 1 - k
-
-        @pl.when(r != me)
-        def _():
-            hop(2, out3, in3, r, r, slot_sem.at[1, r]).wait_recv()
-
-        out4[pl.ds(r * deal, deal)] = later.astype(BF16)
-
-        @pl.when(r != me)
-        def _():
-            hop(3, out4, in4, r, me, all_sem.at[3]).start()
-
-        marks = in1[pl.ds(r * deal, deal)].astype(F32)
-        block = in3[pl.ds(r * deal, deal)].astype(F32)
-        return jnp.where(marks[:, 0:1, :] > 0.0, block, later)
-
-    lax.fori_loop(0, n, hub_back, jnp.zeros((deal, part_rows, width), F32))
-    in4[pl.ds(me * deal, deal)] = mine(out4)
-    whole(2, out3, in3).wait_send()
+    sent(2, out3, in3)
+    told.wait_send()
     for part in range(CHUNKS):
         swaps[part].wait_send()
         back[part].wait_send()
     swap_own.wait()
-    whole(3, out4, in4).wait_recv()
-
-    def give(part, where):
+    store_q.wait()
+    for part in range(deal):
+        lot(3, part, out4, in4).wait_recv()
+
+    def give(part):
         span = pl.ds(part * chunk, chunk)
+        where = dkv_hbm.at[core, span]
         return (
-            pltpu.make_async_copy(total_ref.at[span], where.at[span], store_sem.at[part]),
-            swap(2 * CHUNKS + 1 + part, total_ref.at[span], where.at[span]),
+            pltpu.make_async_copy(total_ref.at[span], where, store_sem.at[part]),
+            swap(2 * CHUNKS + 1 + part, total_ref.at[span], where),
         )
 
     for part in range(CHUNKS):
@@ -392,25 +402,17 @@
             total = own[core, c] + own_rx[c] + jnp.where(slot[c] >= 0, back_rows, 0.0)
             total_ref[c] = total.astype(BF16)
 
-        for which, where in ((0, dk_hbm), (1, dv_hbm)):
-
-            @pl.when(core == which)
-            def _():
-                for copy in give(part, where):
-                    copy.start()
-
-    whole(3, out4, in4).wait_send()
-    told.wait_send()
-    store_q.wait()
-    for part in range(CHUNKS):
-        for which, where, other in ((0, dk_hbm, dv_hbm), (1, dv_hbm, dk_hbm)):
-
-            @pl.when(core == which)
-            def _():
-                here, there = give(part, where)
-                here.wait()
-                there.wait_send()
-                give(part, other)[1].wait_recv()
+        for copy in give(part):
+            copy.start()
+
+    sent(3, out4, in4)
+    for part in range(CHUNKS):
+        for copy in give(part):
+            copy.wait()
+
+
+def pin(x):
+    return pltpu.with_memory_space_constraint(x, pltpu.HBM)
 
 
 def on_device(n, query_heads, key_heads, value_heads, attend_grad, doc_ids, cell_plan):
@@ -426,15 +428,14 @@
     wide = pltpu.VMEM((tokens * heads, width), BF16)
     narrow = pltpu.VMEM((cells, cell, width), BF16)
     n_swaps = 3 * CHUNKS + 1
-    dq, dk, dv = pl.pallas_call(
+    dq, dkv = pl.pallas_call(
         functools.partial(kernel, n, cells, cell, LONG, heads),
         out_shape=(
             jax.ShapeDtypeStruct((tokens * heads, width), BF16),
-            jax.ShapeDtypeStruct((cells, cell, width), BF16),
-            jax.ShapeDtypeStruct((cells, cell, width), BF16),
+            jax.ShapeDtypeStruct((2, cells, cell, width), BF16),
         ),
         in_specs=[hbm] * 6,
-        out_specs=[hbm] * 3,
+        out_specs=[hbm] * 2,
         scratch_shapes=[
             pltpu.SMEM((cells,), jnp.int32),
             pltpu.SMEM((tokens,), jnp.int32),
@@ -453,28 +454,28 @@
             pltpu.VMEM((cells, 8, crow), F32),
             pltpu.VMEM((cells, cell, crow), BF16),
             pltpu.SemaphoreType.DMA((6,)),
-            pltpu.SemaphoreType.DMA((5,)),
-            pltpu.SemaphoreType.DMA((2, n)),
-            pltpu.SemaphoreType.DMA((4,)),
+            pltpu.SemaphoreType.DMA((2,)),
+            pltpu.SemaphoreType.DMA((4, n_slots * PARTS // n)),
+            pltpu.SemaphoreType.DMA((4, n_slots * PARTS // n)),
             pltpu.SemaphoreType.DMA((n_swaps,)),
             pltpu.SemaphoreType.DMA((n_swaps,)),
             pltpu.SemaphoreType.DMA((CHUNKS + 1,)),
         ],
         compiler_params=pltpu.CompilerParams(
-            collective_id=0, has_side_effects=True, vmem_limit_bytes=63 * 2**20
+            collective_id=0, has_side_effects=True, vmem_limit_bytes=48 * 2**20
         ),
     )(
-        cell_plan,
-        doc_ids,
-        query_heads.reshape(tokens * heads, width),
-        key_heads.reshape(cells, cell, width),
-        value_heads.reshape(cells, cell, width),
-        attend_grad.reshape(tokens * heads, width),
+        pin(cell_plan),
+        pin(doc_ids),
+        pin(query_heads.reshape(tokens * heads, width)),
+        pin(key_heads.reshape(cells, cell, width)),
+        pin(value_heads.reshape(cells, cell, width)),
+        pin(attend_grad.reshape(tokens * heads, width)),
     )
     return (
         dq.reshape(tokens, 1, heads, width),
-        dk.reshape(tokens, 1, width),
-        dv.reshape(tokens, 1, width),
+        dkv[0].reshape(tokens, 1, width),
+        dkv[1].reshape(tokens, 1, width),
     )
 
 

time: 73.7 us -> 67 us (0.909)
  Pallas kernels: 68.5 us -> 64.5 us
  local copies, waits for them, and re-layouts: 4.35 us -> 1.79 us
    pallas_call x1, Pallas kernels: 68.5 us -> 64.5 us  [on_device(): pl.pallas_call(functools.partial(kernel, n, cells, cell, LONG, heads), ou...]
    unnamed x7 -> x1, local copies, waits for them, and re-layouts: 4.35 us -> 0.97 us
    slice x0 -> x1, local copies, waits for them, and re-layouts: none -> 0.83 us  [on_device(): dkv[1].reshape(tokens, 1, width)]
where the time goes in v3:
time: 67 us; the launch traced here: 66.9 us
  Pallas kernels  64.5 us (96%)
  local copies, waits for them, and re-layouts  1.79 us (3%)
    pallas_call x1, Pallas kernels, on_device(): pl.pallas_call(functools.partial(kernel, n, cells, cell, LONG, heads), ou...  64.5 us

profile of v3, /device:TPU:1, one launch (start us, length us, event | category | flops | bytes accessed | tf_op | source)
XLA Modules:
  0.0 66.9 jit_solution(584727263627416634)
XLA Ops:
  0.6 64.5 %shard_map.85 = (bf16[4096,128]{1,0:T(8,128)(2,1)S(1)}, bf16[2,16,64,128]{3,2,1,0:T(8,128)(2,1)S(1)}) custom-call(s32[16]{0:T(128)} %plan_hbm.1, s32[1024]{0:T(1024)} %doc_hbm.1, bf16[4096,128]{1,0:T(8,128)(2,1)} %bitcast.10, bf16[16,64,128]{2,1,0:T(8,128)(2,1)} %bitcast.12, bf16[16,64,128]{2,1,0:T(8,128)(2,1)} %bitcast.13, bf16[4096,128]{1,0:T(8,128)(2,1)} %bitcast.11), custom_call_target="tpu_custom_call" | custom-call | tf_op jit(solution)/shard_map/pallas_call | solution.py:431
  65.1 0.8 %fusion = (bf16[1,16,64,128]{3,2,1,0:T(8,128)(2,1)}, bf16[1,16,64,128]{3,2,1,0:T(8,128)(2,1)}) fusion(bf16[2,16,64,128]{3,2,1,0:T(8,128)(2,1)S(1)} %get-tuple-element.6), kind=kLoop, calls=%fused_computation | loop fusion | bytes 1048576 | tf_op jit(solution)/shard_map/slice | solution.py:478
  66.0 1.0 %copy.11 = bf16[1024,1,4,128]{3,2,1,0:T(4,128)(2,1)} copy(bf16[1024,1,4,128]{3,2,1,0:T(4,128)(2,1)S(1)} %bitcast.9) | data formatting | bytes 2097152

commit v4 on v3

v4 whole, which is shorter than its diff:
```python
import functools

import jax
import jax.numpy as jnp
from jax import lax
from jax.experimental import pallas as pl
from jax.experimental.pallas import tpu as pltpu
from jax.sharding import PartitionSpec as P

LONG = 8
CHUNKS = 4
PARTS = 4
RING = 8
MESH = pl.DeviceIdType.MESH
LOG2E = 1.4426950408889634
NEG = -1e30
F32 = jnp.float32
BF16 = jnp.bfloat16
NT = (((1,), (1,)), ((), ()))
TN = (((0,), (0,)), ((), ()))


def dot(a, b, dims=(((1,), (0,)), ((), ()))):
    return lax.dot_general(a, b, dims, preferred_element_type=F32)


def softmax_grads(keys, vals, quer, grad, mask, scale):
    scores = jnp.where(mask, dot(keys, quer, NT), NEG)
    prob_grad = dot(vals, grad, NT)
    top = jnp.max(scores, axis=0, keepdims=True)
    unnorm = jnp.exp2((scores - top) * (scale * LOG2E))
    probs = unnorm * (1.0 / jnp.sum(unnorm, axis=0, keepdims=True))
    delta = jnp.sum(probs * prob_grad, axis=0, keepdims=True)
    dscore = (probs * (prob_grad - delta)).astype(BF16)
    dv = dot(probs.astype(BF16), grad)
    dk = dot(dscore, quer) * scale
    dq = dot(dscore, keys, TN) * scale
    return dq, dk, dv


def kernel(
    n, cells, cell, long_cells, heads,
    plan_hbm, doc_hbm, q_hbm, k_hbm, v_hbm, g_hbm,
    dq_hbm, dkv_hbm,
    plan, doc, flags, rank, slot, inverse, bound, q_ref, k_ref, v_ref, g_ref, dq_ref, total_ref, marked,
    in1, out1, out2, in3, out3, in4, out4,
    prev, dprev, dprev_rx, own, own_rx, stats, final, dscores,
    load_sem, flag_sem, send_sem, recv_sem, sib_send, sib_recv, store_sem,
):
    me = lax.axis_index("dp")
    core = lax.axis_index("section")
    sib = 1 - core
    crow = cell * heads
    width = q_ref.shape[-1]
    scale = width ** -0.5
    chunk = cells // CHUNKS
    part_rows = cell // PARTS
    n_slots = 3 * n // 4
    turns = n_slots * PARTS // n
    per_turn = n_slots // turns
    ring = min(RING, n)
    lines = n // ring
    line_at, ring_at = me // ring, lax.rem(me, ring)

    def peer_of(k):
        turn = k // lines
        odd = lax.rem(turn, 2)
        offset = ring // 2 + odd * (turn + 1) // 2 - (1 - odd) * (turn // 2)
        line = lax.rem(line_at + lines - 1 - lax.rem(k, lines), lines)
        return line * ring + lax.rem(ring_at + offset, ring)

    def each_peer(act):
        def step(k, _):
            act(peer_of(k))
            return 0

        lax.fori_loop(0, n - 1, step, 0, unroll=True)

    loads = [
        pltpu.make_async_copy(src, dst, load_sem.at[i])
        for i, (src, dst) in enumerate(
            ((plan_hbm, plan), (doc_hbm, doc), (k_hbm, k_ref), (v_hbm, v_ref), (q_hbm, q_ref), (g_hbm, g_ref))
        )
    ]
    for load in loads:
        load.start()

    barrier = pltpu.get_barrier_semaphore()

    def greet(peer):
        pl.semaphore_signal(barrier, inc=1, device_id={"dp": peer}, device_id_type=MESH)

    each_peer(greet)
    pl.semaphore_signal(barrier, inc=1, device_id={"section": sib}, device_id_type=MESH)

    def launch(phase, turn, src, dst):
        def send(peer):
            pltpu.make_async_remote_copy(
                src_ref=src.at[turn * n + peer],
                dst_ref=dst.at[turn * n + me],
                send_sem=send_sem.at[phase, turn],
                recv_sem=recv_sem.at[phase, turn],
                device_id={"dp": peer},
                device_id_type=MESH,
            ).start()

        dst[turn * n + me] = src[turn * n + me]
        each_peer(send)

    def lot(phase, turn, src, dst):
        return pltpu.make_async_remote_copy(
            src_ref=src.at[pl.ds(0, n - 1)],
            dst_ref=dst.at[pl.ds(0, n - 1)],
            send_sem=send_sem.at[phase, turn],
            recv_sem=recv_sem.at[phase, turn],
            device_id={"section": sib},
            device_id_type=MESH,
        )

    def sent(phase, src, dst):
        for turn in range(turns):
            lot(phase, turn, src, dst).wait_send()

    def swap(which, src, dst):
        return pltpu.make_async_remote_copy(
            src_ref=src,
            dst_ref=dst,
            send_sem=sib_send.at[which],
            recv_sem=sib_recv.at[which],
            device_id={"section": sib},
            device_id_type=MESH,
        )

    loads[0].wait()
    loads[1].wait()

    def bounds(c, _):
        base = c * cell
        lead = doc[base]
        last = jnp.int32(0)
        step = cell // 2
        while step:
            last = jnp.where(doc[base + last + step] == lead, last + step, last)
            step //= 2
        bound[c] = last + 1
        return 0

    lax.fori_loop(0, cells, bounds, 0, unroll=4)

    for i in range(flags.shape[1]):
        flags[me, i] = plan[0]

    loads[2].wait()
    loads[3].wait()
    row_at = lax.broadcasted_iota(jnp.int32, (cell, width), 0)

    def mark(c, _):
        block = jnp.where(core == 0, k_ref[c], v_ref[c]).astype(F32)
        moved = block
        for i in range(1, PARTS):
            moved = jnp.where(row_at == i, block[i * part_rows : i * part_rows + 1, :], moved)
        moved = jnp.where(row_at % part_rows == 0, bound[c].astype(F32), moved)
        marked[c] = moved.astype(BF16)
        return 0

    lax.fori_loop(0, cells, mark, 0, unroll=4)

    pl.semaphore_wait(barrier, n)

    def tell(peer):
        pltpu.make_async_remote_copy(
            src_ref=flags.at[me],
            dst_ref=flags.at[me],
            send_sem=flag_sem.at[0],
            recv_sem=flag_sem.at[1],
            device_id={"dp": peer},
            device_id_type=MESH,
        ).start()

    each_peer(tell)
    told = pltpu.make_async_remote_copy(
        src_ref=flags.at[pl.ds(0, n - 1)],
        dst_ref=flags.at[pl.ds(0, n - 1)],
        send_sem=flag_sem.at[0],
        recv_sem=flag_sem.at[1],
        device_id={"section": sib},
        device_id_type=MESH,
    )
    loads[4].wait()
    loads[5].wait()
    long_len = long_cells * cell
    own[:, long_cells:] = jnp.zeros((2, cells - long_cells, cell, width), F32)
    dq_ref[long_cells:] = jnp.zeros((cells - long_cells, crow, width), BF16)
    long_key = lax.broadcasted_iota(jnp.int32, (long_len, crow), 0)
    long_query = lax.broadcasted_iota(jnp.int32, (long_len, crow), 1) // heads

    def long_step(c):
        seen = min(2 * (c // 2) + 2, long_cells)
        flat = (seen * cell, width)
        dq, dk, dv = softmax_grads(
            k_ref[:seen].reshape(flat), v_ref[:seen].reshape(flat), q_ref[c], g_ref[c],
            long_key[: seen * cell] <= long_query[: seen * cell] + c * cell, scale,
        )
        dq_ref[c] = dq.astype(BF16)
        for which, grads in ((0, dk), (1, dv)):
            grads = grads.reshape(seen, cell, width)
            if c == long_cells - 1:
                own[which, :seen] = grads
            else:
                own[which, :seen] += grads

    key_at = lax.broadcasted_iota(jnp.int32, (cell, crow), 0)
    query_at = lax.broadcasted_iota(jnp.int32, (cell, crow), 1) // heads
    causal = key_at <= query_at
    query_row = query_at[0:1, :]
    moved_at = jnp.where(key_at < PARTS, key_at * part_rows, key_at)
    moved_at = jnp.where(key_at % part_rows == 0, -1, moved_at)

    def own_block(c):
        low = jnp.where(query_row < bound[c], 0, bound[c])
        scores = jnp.where(causal & (key_at >= low), dot(k_ref[c], q_ref[c], NT), NEG)
        return scores, dot(v_ref[c], g_ref[c], NT)

    def own_stats(c, _):
        scores, prob_grad = own_block(c)
        top = jnp.max(scores, axis=0, keepdims=True)
        unnorm = jnp.exp2((scores - top) * (scale * LOG2E))
        stats[c, 0:1] = top
        stats[c, 1:2] = jnp.sum(unnorm, axis=0, keepdims=True)
        stats[c, 2:3] = jnp.sum(unnorm * prob_grad, axis=0, keepdims=True)
        return 0

    lax.fori_loop(0, cells, own_stats, 0, unroll=4)

    for c in range(long_cells - 1, long_cells - 2, -1):
        long_step(c)
    told.wait_recv()

    keepers = jnp.int32(0)
    for d in range(n):
        rank[d] = d - keepers
        keepers += jnp.where(flags[d, 0] < 0, 1, 0)
    for c in range(cells):
        slot[c] = jnp.where(plan[c] >= 0, rank[jnp.maximum(plan[c], 0)], -1)

    def fill(j, _):
        at = jnp.int32(-1)
        for c in range(cells):
            at = jnp.where(slot[c] == j, c, at)
        inverse[j] = at
        block = jnp.where(at >= 0, marked[jnp.maximum(at, 0)], jnp.zeros((cell, width), BF16))
        out1[pl.ds(j * PARTS, PARTS)] = block.reshape(PARTS, part_rows, width)
        return 0

    lax.fori_loop(0, n_slots, fill, 0, unroll=2)

    for turn in range(turns):
        launch(0, turn, out1, in1)
    for c in range(long_cells - 2, 3, -1):
        long_step(c)

    def hub(turn):
        def step(r, last):
            at = turn * n + r
            out2[at] = last.astype(BF16)
            block = in1[at].astype(F32)
            return jnp.where(block[0:1, :] > 0.0, block, last)

        lax.fori_loop(0, n, step, jnp.zeros((part_rows, width), F32), unroll=8)

    mine = prev.at[core]
    for turn in range(turns):
        lot(0, turn, out1, in1).wait_recv()
        hub(turn)
        launch(1, turn, out2, mine)

    def swap_prev(turn):
        span = pl.ds(turn * n, n)
        return swap(turn, prev.at[core, span], prev.at[core, span])

    def slot_rows(j):
        return pl.ds(j * PARTS, PARTS)

    def cross(j):
        c = jnp.maximum(inverse[j], 0)
        quer, grad = q_ref[c], g_ref[c]
        prev_key = prev[0, slot_rows(j)].reshape(cell, width)
        mark = prev_key.astype(F32)[0:1, :]
        mark = jnp.concatenate([mark] * (crow // width), axis=1)
        mark = jnp.where(mark > 0.0, mark.astype(jnp.int32), cell)
        low = jnp.where(query_row < bound[c], mark, cell)
        scores = jnp.where(moved_at >= low, dot(prev_key, quer, NT), NEG)
        prob_grad = dot(prev[1, slot_rows(j)].reshape(cell, width), grad, NT)
        own_top = stats[c, 0:1]
        top = jnp.maximum(jnp.max(scores, axis=0, keepdims=True), own_top)
        unnorm = jnp.exp2((scores - top) * (scale * LOG2E))
        shrink = jnp.exp2((own_top - top) * (scale * LOG2E))
        inv = 1.0 / (jnp.sum(unnorm, axis=0, keepdims=True) + shrink * stats[c, 1:2])
        delta = inv * (
            jnp.sum(unnorm * prob_grad, axis=0, keepdims=True) + shrink * stats[c, 2:3]
        )
        probs = unnorm * inv
        dscore = (probs * (prob_grad - delta)).astype(BF16)
        final[j, 0:1] = top
        final[j, 1:2] = inv
        final[j, 2:3] = delta
        dscores[j] = dscore
        shape = (PARTS, part_rows, width)
        dprev[0, slot_rows(j)] = (dot(dscore, quer) * scale).astype(BF16).reshape(shape)
        dprev[1, slot_rows(j)] = dot(probs.astype(BF16), grad).astype(BF16).reshape(shape)

    def swap_back(turn):
        span = pl.ds(turn * n, n)
        return swap(turns + turn, dprev.at[sib, span], dprev_rx.at[span])

    def attend(turn):
        swap_prev(turn).wait_recv()
        for j in range(turn * per_turn, (turn + 1) * per_turn):
            cross(j)
        swap_back(turn).start()

    def give_back(turn):
        swap_back(turn).wait_recv()
        span = pl.ds(turn * n, n)
        out3[span] = (dprev[core, span].astype(F32) + dprev_rx[span].astype(F32)).astype(BF16)
        launch(2, turn, out3, in3)

    def own_grads(c, _):
        j = jnp.maximum(slot[c], 0)
        quer, grad = q_ref[c], g_ref[c]
        scores, prob_grad = own_block(c)
        probs = jnp.exp2((scores - final[j, 0:1]) * (scale * LOG2E)) * final[j, 1:2]
        dscore = (probs * (prob_grad - final[j, 2:3])).astype(BF16)
        dv = dot(probs.astype(BF16), grad)
        dk = dot(dscore, quer) * scale
        both = jnp.concatenate([dscores[j], dscore], axis=0)
        keys = jnp.concatenate([prev[0, slot_rows(j)].reshape(cell, width), k_ref[c]], axis=0)
        dq = dot(both, keys, TN) * scale
        kept = plan[c] < 0
        dq_ref[c] = jnp.where(kept, dq_ref[c].astype(F32), dq).astype(BF16)
        own[0, c] = jnp.where(kept, own[0, c], dk)
        own[1, c] = jnp.where(kept, own[1, c], dv)
        return 0

    def hub_back(turn):
        def step(k, later):
            at = turn * n + n - 1 - k
            out4[at] = later.astype(BF16)
            marks = in1[at].astype(F32)
            return jnp.where(marks[0:1, :] > 0.0, in3[at].astype(F32), later)

        lax.fori_loop(0, n, step, jnp.zeros((part_rows, width), F32), unroll=8)

    def pass_back(turn):
        lot(2, turn, out3, in3).wait_recv()
        hub_back(turn)
        launch(3, turn, out4, in4)

    def arrive(turn):
        lot(1, turn, out2, mine).wait_recv()
        swap_prev(turn).start()

    arrive(0)
    for turn in range(turns):
        if turn + 1 < turns:
            arrive(turn + 1)
        attend(turn)
        if turn:
            give_back(turn - 1)
    for c in range(3, -1, -1):
        long_step(c)
    give_back(turns - 1)
    for turn in range(turns):
        pass_back(turn)
        if turn + 1 < turns:
            lax.fori_loop(4 * turn, 4 * turn + 4, own_grads, 0, unroll=4)
    lax.fori_loop(4 * (turns - 1), cells, own_grads, 0, unroll=4)
    swap_own = swap(2 * turns, own.at[sib], own_rx)
    swap_own.start()
    store_q = pltpu.make_async_copy(dq_ref, dq_hbm, store_sem.at[CHUNKS])
    store_q.start()
    sent(0, out1, in1)
    sent(1, out2, mine)
    sent(2, out3, in3)
    told.wait_send()
    for turn in range(turns):
        swap_prev(turn).wait_send()
        swap_back(turn).wait_send()
    swap_own.wait()
    store_q.wait()
    for turn in range(turns):
        lot(3, turn, out4, in4).wait_recv()

    def give(part):
        span = pl.ds(part * chunk, chunk)
        where = dkv_hbm.at[core, span]
        return (
            pltpu.make_async_copy(total_ref.at[span], where, store_sem.at[part]),
            swap(2 * turns + 1 + part, total_ref.at[span], where),
        )

    for part in range(CHUNKS):
        for i in range(chunk):
            c = part * chunk + i
            came = in4[pl.ds(jnp.maximum(slot[c], 0) * PARTS, PARTS)].astype(F32).reshape(cell, width)
            back_rows = jnp.where(row_at < PARTS, 0.0, came)
            for j in range(1, PARTS):
                back_rows = jnp.where(row_at == j * part_rows, came[j : j + 1, :], back_rows)
            total = own[core, c] + own_rx[c] + jnp.where(slot[c] >= 0, back_rows, 0.0)
            total_ref[c] = total.astype(BF16)
        for copy in give(part):
            copy.start()

    sent(3, out4, in4)
    for part in range(CHUNKS):
        for copy in give(part):
            copy.wait()


def pin(x):
    return pltpu.with_memory_space_constraint(x, pltpu.HBM)


def on_device(n, query_heads, key_heads, value_heads, attend_grad, doc_ids, cell_plan):
    tokens, _, heads, width = query_heads.shape
    cells = cell_plan.shape[0]
    cell = tokens // cells
    crow = cell * heads

    n_slots = 3 * n // 4
    slots = pltpu.VMEM((n_slots * PARTS, cell // PARTS, width), BF16)
    both = pltpu.VMEM((2, n_slots * PARTS, cell // PARTS, width), BF16)
    hbm = pl.BlockSpec(memory_space=pl.ANY)
    wide = pltpu.VMEM((cells, crow, width), BF16)
    narrow = pltpu.VMEM((cells, cell, width), BF16)
    n_swaps = 2 * (n_slots * PARTS // n) + 1 + CHUNKS
    dq, dkv = pl.pallas_call(
        functools.partial(kernel, n, cells, cell, LONG, heads),
        out_shape=(
            jax.ShapeDtypeStruct((cells, crow, width), BF16),
            jax.ShapeDtypeStruct((2, cells, cell, width), BF16),
        ),
        in_specs=[hbm] * 6,
        out_specs=[hbm] * 2,
        scratch_shapes=[
            pltpu.SMEM((cells,), jnp.int32),
            pltpu.SMEM((tokens,), jnp.int32),
            pltpu.SMEM((n, 8), jnp.int32),
            pltpu.SMEM((n,), jnp.int32),
            pltpu.SMEM((cells,), jnp.int32),
            pltpu.SMEM((n_slots,), jnp.int32),
            pltpu.SMEM((cells,), jnp.int32),
            wide, narrow, narrow, wide, wide, narrow, narrow,
        ]
        + [slots] * 7
        + [
            both, both, slots,
            pltpu.VMEM((2, cells, cell, width), F32),
            pltpu.VMEM((cells, cell, width), F32),
            pltpu.VMEM((cells, 8, crow), F32),
            pltpu.VMEM((n_slots, 8, crow), F32),
            pltpu.VMEM((n_slots, cell, crow), BF16),
            pltpu.SemaphoreType.DMA((6,)),
            pltpu.SemaphoreType.DMA((2,)),
            pltpu.SemaphoreType.DMA((4, n_slots * PARTS // n)),
            pltpu.SemaphoreType.DMA((4, n_slots * PARTS // n)),
            pltpu.SemaphoreType.DMA((n_swaps,)),
            pltpu.SemaphoreType.DMA((n_swaps,)),
            pltpu.SemaphoreType.DMA((CHUNKS + 1,)),
        ],
        compiler_params=pltpu.CompilerParams(
            collective_id=0, has_side_effects=True, vmem_limit_bytes=48 * 2**20
        ),
    )(
        pin(cell_plan),
        pin(doc_ids),
        pin(query_heads.reshape(cells, crow, width)),
        pin(key_heads.reshape(cells, cell, width)),
        pin(value_heads.reshape(cells, cell, width)),
        pin(attend_grad.reshape(cells, crow, width)),
    )
    return (
        dq.reshape(tokens, 1, heads, width),
        dkv[0].reshape(tokens, 1, width),
        dkv[1].reshape(tokens, 1, width),
    )


def solution(mesh):
    wide = P("dp", "tensor", "section", None)
    narrow = P("dp", "tensor", None)
    return jax.shard_map(
        functools.partial(on_device, mesh.shape["dp"]),
        mesh=mesh,
        in_specs=(wide, narrow, narrow, wide, P("dp"), P("dp")),
        out_specs=(wide, narrow, narrow),
        check_vma=False,
    )
```

time: 67 us -> 63.2 us (0.943)
  Pallas kernels: 64.5 us -> 60.6 us
    pallas_call x1, Pallas kernels: 64.5 us -> 60.6 us  [on_device(): pl.pallas_call(functools.partial(kernel, n, cells, cell, LONG, heads), ou...]
where the time goes in v4:
time: 63.2 us; the launch traced here: 63.1 us
  Pallas kernels  60.6 us (96%)
  local copies, waits for them, and re-layouts  1.79 us (3%)
  between operations  0.64 us (1%)
    pallas_call x1, Pallas kernels, on_device(): pl.pallas_call(functools.partial(kernel, n, cells, cell, LONG, heads), ou...  60.6 us

profile of v4, /device:TPU:1, one launch (start us, length us, event | category | flops | bytes accessed | tf_op | source)
XLA Modules:
  0.0 63.1 jit_solution(12027651367549440466)
XLA Ops:
  0.6 60.6 %shard_map.85 = (bf16[16,256,128]{2,1,0:T(8,128)(2,1)S(1)}, bf16[2,16,64,128]{3,2,1,0:T(8,128)(2,1)S(1)}) custom-call(s32[16]{0:T(128)} %plan_hbm.1, s32[1024]{0:T(1024)} %doc_hbm.1, bf16[16,256,128]{2,1,0:T(8,128)(2,1)} %bitcast.10, bf16[16,64,128]{2,1,0:T(8,128)(2,1)} %bitcast.12, bf16[16,64,128]{2,1,0:T(8,128)(2,1)} %bitcast.13, ...), custom_call_target="tpu_custom_call" | custom-call | tf_op jit(solution)/shard_map/pallas_call | solution.py:437
  61.3 0.8 %fusion = (bf16[1,16,64,128]{3,2,1,0:T(8,128)(2,1)}, bf16[1,16,64,128]{3,2,1,0:T(8,128)(2,1)}) fusion(bf16[2,16,64,128]{3,2,1,0:T(8,128)(2,1)S(1)} %get-tuple-element.6), kind=kLoop, calls=%fused_computation | loop fusion | bytes 1048576 | tf_op jit(solution)/shard_map/slice | solution.py:485
  62.1 1.0 %copy.11 = bf16[1024,1,4,128]{3,2,1,0:T(4,128)(2,1)} copy(bf16[1024,1,4,128]{3,2,1,0:T(4,128)(2,1)S(1)} %bitcast.9) | data formatting | bytes 2097152

commit v5 on v4

--- a/solution.py
+++ b/solution.py
@@ -76,6 +76,14 @@
 
         lax.fori_loop(0, n - 1, step, 0, unroll=True)
 
+    barrier = pltpu.get_barrier_semaphore()
+
+    def greet(peer):
+        pl.semaphore_signal(barrier, inc=1, device_id={"dp": peer}, device_id_type=MESH)
+
+    each_peer(greet)
+    pl.semaphore_signal(barrier, inc=1, device_id={"section": sib}, device_id_type=MESH)
+
     loads = [
         pltpu.make_async_copy(src, dst, load_sem.at[i])
         for i, (src, dst) in enumerate(
@@ -84,14 +92,6 @@
     ]
     for load in loads:
         load.start()
-
-    barrier = pltpu.get_barrier_semaphore()
-
-    def greet(peer):
-        pl.semaphore_signal(barrier, inc=1, device_id={"dp": peer}, device_id_type=MESH)
-
-    each_peer(greet)
-    pl.semaphore_signal(barrier, inc=1, device_id={"section": sib}, device_id_type=MESH)
 
     def launch(phase, turn, src, dst):
         def send(peer):
@@ -132,6 +132,31 @@
         )
 
     loads[0].wait()
+    for i in range(flags.shape[1]):
+        flags[me, i] = plan[0]
+
+    pl.semaphore_wait(barrier, n)
+
+    def tell(peer):
+        pltpu.make_async_remote_copy(
+            src_ref=flags.at[me],
+            dst_ref=flags.at[me],
+            send_sem=flag_sem.at[0],
+            recv_sem=flag_sem.at[1],
+            device_id={"dp": peer},
+            device_id_type=MESH,
+        ).start()
+
+    each_peer(tell)
+    told = pltpu.make_async_remote_copy(
+        src_ref=flags.at[pl.ds(0, n - 1)],
+        dst_ref=flags.at[pl.ds(0, n - 1)],
+        send_sem=flag_sem.at[0],
+        recv_sem=flag_sem.at[1],
+        device_id={"section": sib},
+        device_id_type=MESH,
+    )
+
     loads[1].wait()
 
     def bounds(c, _):
@@ -147,9 +172,6 @@
 
     lax.fori_loop(0, cells, bounds, 0, unroll=4)
 
-    for i in range(flags.shape[1]):
-        flags[me, i] = plan[0]
-
     loads[2].wait()
     loads[3].wait()
     row_at = lax.broadcasted_iota(jnp.int32, (cell, width), 0)
@@ -165,27 +187,6 @@
 
     lax.fori_loop(0, cells, mark, 0, unroll=4)
 
-    pl.semaphore_wait(barrier, n)
-
-    def tell(peer):
-        pltpu.make_async_remote_copy(
-            src_ref=flags.at[me],
-            dst_ref=flags.at[me],
-            send_sem=flag_sem.at[0],
-            recv_sem=flag_sem.at[1],
-            device_id={"dp": peer},
-            device_id_type=MESH,
-        ).start()
-
-    each_peer(tell)
-    told = pltpu.make_async_remote_copy(
-        src_ref=flags.at[pl.ds(0, n - 1)],
-        dst_ref=flags.at[pl.ds(0, n - 1)],
-        send_sem=flag_sem.at[0],
-        recv_sem=flag_sem.at[1],
-        device_id={"section": sib},
-        device_id_type=MESH,
-    )
     loads[4].wait()
     loads[5].wait()
     long_len = long_cells * cell
@@ -361,20 +362,22 @@
         swap_prev(turn).start()
 
     arrive(0)
-    for turn in range(turns):
-        if turn + 1 < turns:
-            arrive(turn + 1)
-        attend(turn)
-        if turn:
-            give_back(turn - 1)
+    attend(0)
+    arrive(1)
+    give_back(0)
+    attend(1)
+    arrive(2)
+    give_back(1)
+    attend(2)
+    give_back(2)
     for c in range(3, -1, -1):
         long_step(c)
-    give_back(turns - 1)
-    for turn in range(turns):
-        pass_back(turn)
-        if turn + 1 < turns:
-            lax.fori_loop(4 * turn, 4 * turn + 4, own_grads, 0, unroll=4)
-    lax.fori_loop(4 * (turns - 1), cells, own_grads, 0, unroll=4)
+    pass_back(0)
+    lax.fori_loop(0, 4, own_grads, 0, unroll=4)
+    pass_back(1)
+    lax.fori_loop(4, 8, own_grads, 0, unroll=4)
+    pass_back(2)
+    lax.fori_loop(8, 16, own_grads, 0, unroll=4)
     swap_own = swap(2 * turns, own.at[sib], own_rx)
     swap_own.start()
     store_q = pltpu.make_async_copy(dq_ref, dq_hbm, store_sem.at[CHUNKS])
@@ -388,6 +391,12 @@
         swap_back(turn).wait_send()
     swap_own.wait()
     store_q.wait()
+
+    def settle(c, _):
+        own_rx[c] += own[core, c]
+        return 0
+
+    lax.fori_loop(0, cells, settle, 0, unroll=4)
     for turn in range(turns):
         lot(3, turn, out4, in4).wait_recv()
 
@@ -406,7 +415,7 @@
             back_rows = jnp.where(row_at < PARTS, 0.0, came)
             for j in range(1, PARTS):
                 back_rows = jnp.where(row_at == j * part_rows, came[j : j + 1, :], back_rows)
-            total = own[core, c] + own_rx[c] + jnp.where(slot[c] >= 0, back_rows, 0.0)
+            total = own_rx[c] + jnp.where(slot[c] >= 0, back_rows, 0.0)
             total_ref[c] = total.astype(BF16)
         for copy in give(part):
             copy.start()

time: 63.2 us -> 61.9 us (0.979)
  Pallas kernels: 60.6 us -> 59.3 us
    pallas_call x1, Pallas kernels: 60.6 us -> 59.3 us  [on_device(): pl.pallas_call(functools.partial(kernel, n, cells, cell, LONG, heads), ou...]
where the time goes in v5:
time: 61.9 us; the launch traced here: 61.8 us
  Pallas kernels  59.3 us (96%)
  local copies, waits for them, and re-layouts  1.79 us (3%)
  between operations  0.64 us (1%)
    pallas_call x1, Pallas kernels, on_device(): pl.pallas_call(functools.partial(kernel, n, cells, cell, LONG, heads), ou...  59.3 us

profile of v5, /device:TPU:1, one launch (start us, length us, event | category | flops | bytes accessed | tf_op | source)
XLA Modules:
  0.0 61.8 jit_solution(9984608809413594782)
XLA Ops:
  0.6 59.3 %shard_map.85 = (bf16[16,256,128]{2,1,0:T(8,128)(2,1)S(1)}, bf16[2,16,64,128]{3,2,1,0:T(8,128)(2,1)S(1)}) custom-call(s32[16]{0:T(128)} %plan_hbm.1, s32[1024]{0:T(1024)} %doc_hbm.1, bf16[16,256,128]{2,1,0:T(8,128)(2,1)} %bitcast.10, bf16[16,64,128]{2,1,0:T(8,128)(2,1)} %bitcast.12, bf16[16,64,128]{2,1,0:T(8,128)(2,1)} %bitcast.13, ...), custom_call_target="tpu_custom_call" | custom-call | tf_op jit(solution)/shard_map/pallas_call | solution.py:446
  60.0 0.8 %fusion = (bf16[1,16,64,128]{3,2,1,0:T(8,128)(2,1)}, bf16[1,16,64,128]{3,2,1,0:T(8,128)(2,1)}) fusion(bf16[2,16,64,128]{3,2,1,0:T(8,128)(2,1)S(1)} %get-tuple-element.6), kind=kLoop, calls=%fused_computation | loop fusion | bytes 1048576 | tf_op jit(solution)/shard_map/slice | solution.py:494
  60.8 1.0 %copy.11 = bf16[1024,1,4,128]{3,2,1,0:T(4,128)(2,1)} copy(bf16[1024,1,4,128]{3,2,1,0:T(4,128)(2,1)S(1)} %bitcast.9) | data formatting | bytes 2097152

commit v6 on v5

--- a/solution.py
+++ b/solution.py
@@ -253,11 +253,11 @@
         out1[pl.ds(j * PARTS, PARTS)] = block.reshape(PARTS, part_rows, width)
         return 0
 
-    lax.fori_loop(0, n_slots, fill, 0, unroll=2)
 
     for turn in range(turns):
+        lax.fori_loop(turn * per_turn, (turn + 1) * per_turn, fill, 0, unroll=2)
         launch(0, turn, out1, in1)
-    for c in range(long_cells - 2, 3, -1):
+    for c in range(long_cells - 2, -1, -1):
         long_step(c)
 
     def hub(turn):
@@ -370,8 +370,6 @@
     give_back(1)
     attend(2)
     give_back(2)
-    for c in range(3, -1, -1):
-        long_step(c)
     pass_back(0)
     lax.fori_loop(0, 4, own_grads, 0, unroll=4)
     pass_back(1)

time: 61.9 us -> 61.6 us (level)
  no operation moved by 1% of the time
where the time goes in v6:
time: 61.6 us; the launch traced here: 61.5 us
  Pallas kernels  59.1 us (96%)
  local copies, waits for them, and re-layouts  1.79 us (3%)
  between operations  0.64 us (1%)
    pallas_call x1, Pallas kernels, on_device(): pl.pallas_call(functools.partial(kernel, n, cells, cell, LONG, heads), ou...  59.1 us

profile of v6, /device:TPU:1, one launch (start us, length us, event | category | flops | bytes accessed | tf_op | source)
XLA Modules:
  0.0 61.5 jit_solution(12692349917681528088)
XLA Ops:
  0.6 59.1 %shard_map.85 = (bf16[16,256,128]{2,1,0:T(8,128)(2,1)S(1)}, bf16[2,16,64,128]{3,2,1,0:T(8,128)(2,1)S(1)}) custom-call(s32[16]{0:T(128)} %plan_hbm.1, s32[1024]{0:T(1024)} %doc_hbm.1, bf16[16,256,128]{2,1,0:T(8,128)(2,1)} %bitcast.10, bf16[16,64,128]{2,1,0:T(8,128)(2,1)} %bitcast.12, bf16[16,64,128]{2,1,0:T(8,128)(2,1)} %bitcast.13, ...), custom_call_target="tpu_custom_call" | custom-call | tf_op jit(solution)/shard_map/pallas_call | solution.py:444
  59.7 0.8 %fusion = (bf16[1,16,64,128]{3,2,1,0:T(8,128)(2,1)}, bf16[1,16,64,128]{3,2,1,0:T(8,128)(2,1)}) fusion(bf16[2,16,64,128]{3,2,1,0:T(8,128)(2,1)S(1)} %get-tuple-element.6), kind=kLoop, calls=%fused_computation | loop fusion | bytes 1048576 | tf_op jit(solution)/shard_map/slice | solution.py:492
  60.6 1.0 %copy.11 = bf16[1024,1,4,128]{3,2,1,0:T(4,128)(2,1)} copy(bf16[1024,1,4,128]{3,2,1,0:T(4,128)(2,1)S(1)} %bitcast.9) | data formatting | bytes 2097152
